TPU v7x, 32 devices: a whole 2x2x4 slice. The times are simulated.
32 devices in a mesh: gy: 4 (over y, x), gz: 8 (over z, core).
Axes of the slice: x: 2, y: 2, z: 4, core: 2. Of those that a mesh axis runs over, the one named last changes fastest.
Arguments:
- density: float32 [32, 96, 1024], P(None, 'gy', 'gz'), may hold values from 1 to 2
- momentum: float32 [3, 32, 96, 1024], P(None, None, 'gy', 'gz'), may hold values from -0.5 to 0.5
- energy: float32 [32, 96, 1024], P(None, 'gy', 'gz'), may hold values from 3 to 5
Outputs:
- density_out: float32 [32, 96, 1024], P(None, 'gy', 'gz')
- momentum_out: float32 [3, 32, 96, 1024], P(None, None, 'gy', 'gz')
- energy_out: float32 [32, 96, 1024], P(None, 'gy', 'gz')
All inputs are finite; a program needn't handle non-finite values.
Results may differ from a plain program's by a relative error of at most 0.0003.
Values sent between devices are 32-bit elements; how exact they have to be, the bound alone decides.
No kernel may reach another device: no remote copies, remote signals or barrier semaphores. Data moves between devices by JAX's collectives and lax.ppermute only.
A program may use at most 64 MiB of HBM per device.

v0:
```python
import functools

import jax
import jax.numpy as jnp
from jax import lax
from jax.experimental import pallas as pl
from jax.experimental.pallas import tpu as pltpu
from jax.sharding import PartitionSpec as P

adiabatic = 1.4
courant = 0.15
halo = 3
quarters = 4


def primitives(fields):
    density, mx, my, mz, energy = fields
    inverse = pl.reciprocal(density, approx=True)
    vx, vy, vz = mx * inverse, my * inverse, mz * inverse
    doubled = mx * vx + my * vy + mz * vz
    pressure = (adiabatic - 1.0) * energy - (0.5 * (adiabatic - 1.0)) * doubled
    return [density, vx, vy, vz, pressure]


def half_slope(ahead, behind):
    top = jnp.maximum(jnp.minimum(ahead, behind), 0.0)
    bottom = jnp.minimum(jnp.maximum(ahead, behind), 0.0)
    return jnp.maximum(jnp.minimum(0.25 * (ahead + behind), top), bottom)


def face_offset(ahead, slope, slope_next):
    offset = 0.5 * ahead - (1.0 / 3.0) * (slope_next - slope)
    return jnp.minimum(jnp.maximum(offset, jnp.minimum(ahead, 0.0)), jnp.maximum(ahead, 0.0))


def limited(first, second):
    doubled = second + second
    return jnp.maximum(jnp.minimum(first, jnp.maximum(doubled, 0.0)), jnp.minimum(doubled, 0.0))


def hll(left, right, normal):
    dl, pl_, ul = left[0], left[4], left[1 + normal]
    dr, pr, ur = right[0], right[4], right[1 + normal]
    tl = adiabatic * pl_
    tr = adiabatic * pr
    al = tl * lax.rsqrt(tl * dl)
    ar = tr * lax.rsqrt(tr * dr)
    slowest = jnp.minimum(jnp.minimum(ul - al, ur - ar), 0.0)
    fastest = jnp.maximum(jnp.maximum(ul + al, ur + ar), 0.0)
    cl = fastest * (courant * pl.reciprocal(fastest - slowest, approx=True))
    cr = courant - cl
    wl = cl * (ul - slowest)
    wr = cr * (ur - fastest)
    ml = wl * dl
    mr = wr * dr
    ql = cl * pl_
    qr = cr * pr
    gl = [ml * left[1 + k] for k in range(3)]
    gr = [mr * right[1 + k] for k in range(3)]
    kinetic = (
        gl[0] * left[1] + gl[1] * left[2] + gl[2] * left[3]
        + gr[0] * right[1] + gr[1] * right[2] + gr[2] * right[3]
    )
    flux = [ml + mr] + [gl[k] + gr[k] for k in range(3)]
    flux[1 + normal] = flux[1 + normal] + (ql + qr)
    inner = (1.0 / (adiabatic - 1.0)) * (wl * pl_ + wr * pr)
    flux.append(0.5 * kinetic + inner + (ql * ul + qr * ur))
    return flux


class Line:
    def __init__(self, load, normal, period=None):
        self.load, self.normal, self.period = load, normal, period
        self.known = {}

    def once(self, name, index, make):
        if self.period is not None:
            index = index % self.period
        if (name, index) not in self.known:
            self.known[(name, index)] = make(index)
        return self.known[(name, index)]

    def prims(self, i):
        return self.once("q", i, lambda i: primitives(self.load(i)))

    def diff(self, i):
        return self.once("d", i, lambda i: [b - a for a, b in zip(self.prims(i), self.prims(i + 1))])

    def slope(self, i):
        return self.once("s", i, lambda i: [half_slope(a, b) for a, b in zip(self.diff(i), self.diff(i - 1))])

    def up(self, i):
        return self.once("u", i, lambda i: [face_offset(d, s, t) for d, s, t in zip(self.diff(i), self.slope(i), self.slope(i + 1))])

    def down(self, i):
        return self.once("w", i, lambda i: [d - u for d, u in zip(self.diff(i - 1), self.up(i - 1))])

    def low(self, i):
        return self.once("l", i, lambda i: [q - limited(w, u) for q, w, u in zip(self.prims(i), self.down(i), self.up(i))])

    def high(self, i):
        return self.once("h", i, lambda i: [q + limited(u, w) for q, w, u in zip(self.prims(i), self.down(i), self.up(i))])

    def flux(self, i):
        return self.once("f", i, lambda i: hll(self.high(i), self.low(i + 1), self.normal))

    def swept(self, i):
        before, after = self.flux(i - 1), self.flux(i)
        return [u - (b - a) for u, a, b in zip(self.load(i), before, after)]


def rolled(fields, ahead, behind, normal):
    states = primitives(fields)
    low, high = [], []
    for q in states:
        d = ahead(q) - q
        s = half_slope(d, behind(d))
        u = face_offset(d, s, ahead(s))
        w = behind(d - u)
        low.append(ahead(q - limited(w, u)))
        high.append(q + limited(u, w))
    return hll(high, low, normal)


def shifts(axis, size):
    return (lambda a: pltpu.roll(a, size - 1, axis), lambda a: pltpu.roll(a, 1, axis))


def row(index):
    return pl.ds(index, 8)


def fields_of(density, momentum, energy):
    return [density, momentum.at[0], momentum.at[1], momentum.at[2], energy]


def odd_rank(axis):
    return lax.axis_index(axis) % 2 == 1


class Received:
    def __init__(self, odd, on_odd, on_even):
        self.odd, self.on_odd, self.on_even = odd, on_odd, on_even

    def __getitem__(self, index):
        return jnp.where(self.odd, self.on_odd[index], self.on_even[index])


def sides_of(axis, far, near):
    odd = odd_rank(axis)
    return Received(odd, near, far), Received(odd, far, near)


def rows_kernel(density, momentum, energy, far, near, held, arrived):
    sources = fields_of(density, momentum, energy)
    nx, ny, nz = density.shape
    copies = []
    for f in range(5):
        for side in range(2):
            tile = sources[f].at[:, pl.ds(side * (ny - 8), 8), :]
            copies.append(pltpu.make_async_copy(tile, held.at[side, f], arrived.at[side, f]))
    for copy in copies:
        copy.start()
    odd = odd_rank("gy")
    for f in range(5):
        copies[2 * f].wait()
        copies[2 * f + 1].wait()
        top, bottom = (held.at[side, f].reshape(nx * 8, nz) for side in range(2))
        for r in range(halo):
            first = top[pl.ds(r, nx, stride=8), :]
            last = bottom[pl.ds(8 - halo + r, nx, stride=8), :]
            far[f, r] = jnp.where(odd, last, first)
            near[f, r] = jnp.where(odd, first, last)


def turn_in(source, turned, count):
    lanes = source.shape[-1]
    span = lanes // quarters

    @pl.loop(0, 5)
    def _(f):
        for b in range(count):
            block = source[f, pl.ds(b * lanes, lanes), :].T
            for q in range(quarters):
                turned[f, pl.ds(q * count + b, span, stride=quarters * count), :] = block[q * span : (q + 1) * span]


def turn_out(turned, count, store):
    lanes = turned.shape[-1]
    span = lanes // quarters
    for f in range(5):
        for b in range(count):
            parts = [turned[f, pl.ds(q * count + b, span, stride=quarters * count), :] for q in range(quarters)]
            store(f, b, jnp.concatenate(parts, axis=0).T)


def ends(turned, count, far, near):
    span = turned.shape[1] // (quarters * count)
    odd = odd_rank("gz")
    for f in range(5):
        for k in range(halo):
            upward = turned[f, row((span - halo + k + 1) * quarters * count - 8), :]
            downward = turned[f, row(k * quarters * count), :]
            far[f, k] = jnp.where(odd, upward, downward)
            near[f, k] = jnp.where(odd, downward, upward)


def z_sweep(own, far, near, swept, count):
    left, right = sides_of("gz", far, near)
    width = quarters * count
    span = own.shape[1] // width
    place = lax.broadcasted_iota(jnp.int32, (8, own.shape[-1]), 0)
    for start in range(0, width, 8):

        def load(i):
            if 0 <= i < span:
                return [own[f, row(i * width + start), :] for f in range(5)]
            if i < 0:
                fields = [own[f, row((i + span) * width + start - count), :] for f in range(5)]
                if start == 0:
                    fields = [jnp.where(place < count, pltpu.roll(left[f, i + halo], count, 0), a) for f, a in enumerate(fields)]
                return fields
            fields = [own[f, row((i - span) * width + start + count), :] for f in range(5)]
            if start + 8 == width:
                fields = [jnp.where(place >= 8 - count, pltpu.roll(right[f, i - span], 8 - count, 0), a) for f, a in enumerate(fields)]
            return fields

        line = Line(load, 2)
        for i in range(span):
            for f, value in enumerate(line.swept(i)):
                swept[f, row(i * width + start), :] = value


def inner_kernel(density, momentum, energy, turned, far, near, rim, joint, held, inner):
    nx, ny, lanes = density.shape
    deep = lanes // nx
    sources = fields_of(density, momentum, energy)

    @pl.loop(0, ny // 8)
    def _(tile):
        start = pl.multiple_of(tile * 8, 8)
        line = Line(lambda i: [s[i, pl.ds(start, 8), :] for s in sources], 0, nx)
        for i in range(nx):
            for f, value in enumerate(line.swept(i)):
                held[f, pl.ds(pl.multiple_of(i * ny + start, 8), 8), :] = value

    @pl.loop(0, nx // 8)
    def _(tile):
        some = pl.ds(pl.multiple_of(tile * 8, 8), 8)
        line = Line(lambda i: [held[f, pl.ds(tile * (8 * ny) + i, 8, stride=ny), :] for f in range(5)], 1)
        for i in range(deep, ny - deep):
            for f, value in enumerate(line.swept(i)):
                inner[f, pl.ds(pl.multiple_of((i - deep) * nx + tile * 8, 8), 8), :] = value
        for f in range(5):
            joint[f, 0, some, :] = line.flux(deep - 1)[f]
            joint[f, 1, some, :] = line.flux(ny - deep - 1)[f]
        kept = deep + halo - 1
        for r in range(kept):
            for f, (a, b) in enumerate(zip(line.load(r), line.load(ny - kept + r))):
                rim[f, r, some, :] = a
                rim[f, kept + r, some, :] = b

    count = ny // deep - 2
    turn_in(inner, turned, count)
    ends(turned, count, far, near)


def edge_kernel(far, near, rim, joint, _, turned, far_end, near_end, ghost, outer):
    _, kept, nx, lanes = rim.shape
    kept = kept // 2
    deep = lanes // nx
    ahead, behind = shifts(0, nx)
    for side, source in enumerate(sides_of("gy", far, near)):

        @pl.loop(0, halo)
        def _(r):
            fields = [source[f, r] for f in range(5)]
            flux = rolled(fields, ahead, behind, 0)
            for f in range(5):
                ghost[f, side * halo + r] = fields[f] - (flux[f] - behind(flux[f]))

    @pl.loop(0, nx // 8)
    def _(tile):
        some = pl.ds(pl.multiple_of(tile * 8, 8), 8)
        for side in range(2):

            def load(i):
                if side == 0:
                    source, at = (ghost, i + halo) if i < 0 else (rim, i)
                else:
                    source, at = (ghost, i - deep + halo) if i >= deep else (rim, i + kept + kept - deep)
                return [source[f, at, some, :] for f in range(5)]

            line = Line(load, 1)
            known = deep - 1 if side == 0 else -1
            line.known[("f", known)] = [joint[f, side, some, :] for f in range(5)]
            for i in range(deep):
                for f, value in enumerate(line.swept(i)):
                    outer[f, pl.ds(pl.multiple_of((side * deep + i) * nx + tile * 8, 8), 8), :] = value

    turn_in(outer, turned, 2)
    ends(turned, 2, far_end, near_end)


def inner_z_kernel(count, own, far, near, out, swept):
    lanes = own.shape[-1]
    z_sweep(own, far, near, swept, count)

    def store(f, b, block):
        out[f, pl.ds(b * lanes, lanes), :] = block

    turn_out(swept, count, store)


def edge_z_kernel(ny, own, far, near, inner, density, momentum, energy, swept):
    lanes = own.shape[-1]
    nx = density.shape[0] // ny
    deep = lanes // nx
    outs = fields_of(density, momentum, energy)
    z_sweep(own, far, near, swept, 2)
    for f in range(5):
        for i in range(deep, ny - deep):
            outs[f][pl.ds(i, nx, stride=ny), :] = inner[f, pl.ds((i - deep) * nx, nx), :]

    def store(f, b, block):
        for r in range(deep):
            outs[f][pl.ds(b * (ny - deep) + r, nx, stride=ny), :] = block[r * nx : (r + 1) * nx]

    turn_out(swept, 2, store)


def call(kernel, shapes, scratch, arguments, in_specs=None):
    whole = pl.BlockSpec(memory_space=pltpu.VMEM)
    return pl.pallas_call(
        kernel,
        out_shape=[jax.ShapeDtypeStruct(shape, jnp.float32) for shape in shapes],
        in_specs=[whole] * len(arguments) if in_specs is None else in_specs,
        out_specs=[whole] * len(shapes),
        scratch_shapes=[pltpu.VMEM(shape, jnp.float32) for shape in scratch],
        compiler_params=pltpu.CompilerParams(vmem_limit_bytes=24 * 2**20),
    )(*arguments)


def exchange(axis, far, near):
    ranks = lax.axis_size(axis)
    if ranks % 2:
        raise ValueError("odd ring")
    pairs = []
    for start in (1, 0):
        there = [(rank, (rank + 1) % ranks) for rank in range(start, ranks, 2)]
        pairs.append(there + [(b, a) for a, b in there])
    return lax.ppermute(far, axis, pairs[0]), lax.ppermute(near, axis, pairs[1])


def y_rows(density, momentum, energy):
    nx, ny, nz = density.shape
    shape = (5, halo, nx, nz)
    return pl.pallas_call(
        rows_kernel,
        out_shape=[pltpu.VMEM(shape, jnp.float32)] * 2,
        in_specs=[pl.BlockSpec(memory_space=pltpu.HBM)] * 3,
        out_specs=[pl.BlockSpec(memory_space=pltpu.VMEM)] * 2,
        scratch_shapes=[pltpu.VMEM((2, 5, nx, 8, nz), jnp.float32), pltpu.SemaphoreType.DMA((2, 5))],
        compiler_params=pltpu.CompilerParams(vmem_limit_bytes=16 * 2**20),
    )(*(pltpu.with_memory_space_constraint(a, pltpu.HBM) for a in (density, momentum, energy)))


def body(density, momentum, energy):
    nx, ny, nz = density.shape
    deep = nz // nx
    count = ny // deep - 2
    kept = deep + halo - 1
    end = (5, halo, 8, nz)

    far_rows, near_rows = exchange("gy", *y_rows(density, momentum, energy))
    turned, far, near, rim, joint = call(
        inner_kernel,
        [(5, count * nz, nz), end, end, (5, 2 * kept, nx, nz), (5, 2, nx, nz)],
        [(5, nx * ny, nz), (5, count * nz, nz)],
        [density, momentum, energy],
    )
    far, near = exchange("gz", far, near)
    (inner,) = call(
        functools.partial(inner_z_kernel, count),
        [(5, count * nz, nz)],
        [(5, count * nz, nz)],
        [turned, far, near],
    )
    whole = pl.BlockSpec(memory_space=pltpu.VMEM)
    turned, far, near = call(
        edge_kernel,
        [(5, 2 * nz, nz), end, end],
        [(5, 2 * halo, nx, nz), (5, 2 * nz, nz)],
        [far_rows, near_rows, rim, joint, inner],
        [whole] * 4 + [pl.BlockSpec(memory_space=pl.ANY)],
    )
    far, near = exchange("gz", far, near)
    cells = nx * ny
    outs = call(
        functools.partial(edge_z_kernel, ny),
        [(cells, nz), (3, cells, nz), (cells, nz)],
        [(5, 2 * nz, nz)],
        [turned, far, near, inner],
    )
    return (outs[0].reshape(nx, ny, nz), outs[1].reshape(3, nx, ny, nz), outs[2].reshape(nx, ny, nz))


def solution(mesh):
    return jax.shard_map(
        body,
        mesh=mesh,
        in_specs=(P(None, "gy", "gz"), P(None, None, "gy", "gz"), P(None, "gy", "gz")),
        out_specs=(P(None, "gy", "gz"), P(None, None, "gy", "gz"), P(None, "gy", "gz")),
        check_vma=False,
    )
```

profile of v0, /device:TPU:0, one launch (start us, length us, event | category | flops | bytes accessed | tf_op | source)
XLA Modules:
  0.0 33.2 jit_solution(8856772319168753323)
XLA Ops:
  0.6 0.0 copy-start.1
  0.6 0.0 copy-start
  0.7 0.0 copy-start.2
  0.7 1.6 %shard_map.58 = (f32[5,3,32,128]{3,2,1,0:T(8,128)S(1)}, f32[5,3,32,128]{3,2,1,0:T(8,128)S(1)}) custom-call(f32[32,24,128]{2,1,0:T(8,128)} %density.3, f32[3,32,24,128]{3,2,1,0:T(8,128)} %momentum.3, f32[32,24,128]{2,1,0:T(8,128)} %energy.3), custom_call_target="tpu_custom_call" | custom-call | tf_op jit(solution)/shard_map/pallas_call | solution.py:358
  2.3 4.0 %collective-permute-start = (f32[5,3,32,128]{3,2,1,0:T(8,128)S(1)}, f32[5,3,32,128]{3,2,1,0:T(8,128)S(1)}, u32[]{:S(2)}, u32[]{:S(2)}) collective-permute-start(f32[5,3,32,128]{3,2,1,0:T(8,128)S(1)} %get-tuple-element.16), channel_id=1, source_target_pairs={{8,16},{24,0},{16,8},{0,24},{9,17},{25,1},{17,9},{1,25},{10,18},{2... | collective-permute-start | bytes 737288 | tf_op jit(solution)/shard_map/ppermute | solution.py:352
  6.2 0.5 %collective-permute-start.1 = (f32[5,3,32,128]{3,2,1,0:T(8,128)S(1)}, f32[5,3,32,128]{3,2,1,0:T(8,128)S(1)}, u32[]{:S(2)}, u32[]{:S(2)}) collective-permute-start(f32[5,3,32,128]{3,2,1,0:T(8,128)S(1)} %get-tuple-element.17), channel_id=1, source_target_pairs={{0,8},{16,24},{8,0},{24,16},{1,9},{17,25},{9,1},{25,17},{2,10},{18... | collective-permute-start | bytes 737288 | tf_op jit(solution)/shard_map/ppermute | solution.py:352
  6.8 0.0 copy-done.1
  6.8 0.0 copy-done
  6.8 0.0 copy-done.2
  6.8 6.5 %shard_map.59 = (f32[5,512,128]{2,1,0:T(8,128)S(1)}, f32[5,3,8,128]{3,2,1,0:T(8,128)S(1)}, f32[5,3,8,128]{3,2,1,0:T(8,128)S(1)}, f32[5,12,32,128]{3,2,1,0:T(8,128)S(1)}, f32[5,2,32,128]{3,2,1,0:T(8,128)S(1)}) custom-call(f32[32,24,128]{2,1,0:T(8,128)S(1)} %copy-done.1, f32[3,32,24,128]{3,2,1,0:T(8,128)S(1)} %copy-done, f32[32,24,128]{2,1,0:T(8,128)S(1)} %copy-done.2), custom_call_target="tpu_custom_call" | custom-call | tf_op jit(solution)/shard_map/pallas_call | solution.py:334
  13.3 2.5 %collective-permute-start.2 = (f32[5,3,8,128]{3,2,1,0:T(8,128)S(1)}, f32[5,3,8,128]{3,2,1,0:T(8,128)S(1)}, u32[]{:S(2)}, u32[]{:S(2)}) collective-permute-start(f32[5,3,8,128]{3,2,1,0:T(8,128)S(1)} %get-tuple-element.21), channel_id=1, source_target_pairs={{1,2},{3,4},{5,6},{7,0},{2,1},{4,3},{6,5},{0,7},{9,10},{11,12},{13... | collective-permute-start | bytes 184328 | tf_op jit(solution)/shard_map/ppermute | solution.py:352
  15.9 0.0 collective-permute-start.3
  15.9 3.3 %collective-permute-done.2.far = f32[5,3,8,128]{3,2,1,0:T(8,128)S(1)} collective-permute-done((f32[5,3,8,128]{3,2,1,0:T(8,128)S(1)}, f32[5,3,8,128]{3,2,1,0:T(8,128)S(1)}, u32[]{:S(2)}, u32[]{:S(2)}) %collective-permute-start.2) | collective-permute-done | bytes 61472 | tf_op jit(solution)/shard_map/ppermute | solution.py:352
  19.2 0.0 collective-permute-done.3.near
  19.2 2.7 %shard_map.60._.inner = f32[5,512,128]{2,1,0:T(8,128)S(1)} custom-call(f32[5,512,128]{2,1,0:T(8,128)S(1)} %get-tuple-element.20.own, f32[5,3,8,128]{3,2,1,0:T(8,128)S(1)} %collective-permute-done.2.far, f32[5,3,8,128]{3,2,1,0:T(8,128)S(1)} %collective-permute-done.3.near), custom_call_target="tpu_custom_call" | custom-call | tf_op jit(solution)/shard_map/pallas_call | solution.py:334
  22.0 0.0 collective-permute-done.far
  22.0 0.0 collective-permute-done.1.near
  22.0 3.0 %shard_map.61 = (f32[5,256,128]{2,1,0:T(8,128)S(1)}, f32[5,3,8,128]{3,2,1,0:T(8,128)S(1)}, f32[5,3,8,128]{3,2,1,0:T(8,128)S(1)}) custom-call(f32[5,3,32,128]{3,2,1,0:T(8,128)S(1)} %collective-permute-done.far, f32[5,3,32,128]{3,2,1,0:T(8,128)S(1)} %collective-permute-done.1.near, f32[5,12,32,128]{3,2,1,0:T(8,128)S(1)} %get-tuple-element.18.rim, ...), custom_call_target="tpu_custom_call" | custom-call | tf_op jit(solution)/shard_map/pallas_call | solution.py:334
  25.0 2.2 %collective-permute-start.4 = (f32[5,3,8,128]{3,2,1,0:T(8,128)S(1)}, f32[5,3,8,128]{3,2,1,0:T(8,128)S(1)}, u32[]{:S(2)}, u32[]{:S(2)}) collective-permute-start(f32[5,3,8,128]{3,2,1,0:T(8,128)S(1)} %get-tuple-element.24), channel_id=1, source_target_pairs={{1,2},{3,4},{5,6},{7,0},{2,1},{4,3},{6,5},{0,7},{9,10},{11,12},{13... | collective-permute-start | bytes 184328 | tf_op jit(solution)/shard_map/ppermute | solution.py:352
  27.1 0.0 collective-permute-start.5
  27.1 3.3 %collective-permute-done.4.far = f32[5,3,8,128]{3,2,1,0:T(8,128)S(1)} collective-permute-done((f32[5,3,8,128]{3,2,1,0:T(8,128)S(1)}, f32[5,3,8,128]{3,2,1,0:T(8,128)S(1)}, u32[]{:S(2)}, u32[]{:S(2)}) %collective-permute-start.4) | collective-permute-done | bytes 61472 | tf_op jit(solution)/shard_map/ppermute | solution.py:352
  30.5 0.0 collective-permute-done.5.near
  30.5 2.7 %shard_map.62 = (f32[768,128]{1,0:T(8,128)}, f32[3,768,128]{2,1,0:T(8,128)}, f32[768,128]{1,0:T(8,128)}) custom-call(f32[5,256,128]{2,1,0:T(8,128)S(1)} %get-tuple-element.23.own, f32[5,3,8,128]{3,2,1,0:T(8,128)S(1)} %collective-permute-done.4.far, f32[5,3,8,128]{3,2,1,0:T(8,128)S(1)} %collective-permute-done.5.near, f32[5,512,128]{2,1,0:T(8,128)S(1)} %shard_map.60._.inner), custom_call_target="tpu_custom_call" | custom-call | tf_op jit(solution)/shard_map/pallas_call | solution.py:334
Async XLA Ops:
  0.6 6.1 %copy-start.1 = (f32[32,24,128]{2,1,0:T(8,128)S(1)}, f32[32,24,128]{2,1,0:T(8,128)}, u32[]{:S(2)}) copy-start(f32[32,24,128]{2,1,0:T(8,128)} %density.3) | copy-start | bytes 1179652
  0.6 6.1 %copy-start = (f32[3,32,24,128]{3,2,1,0:T(8,128)S(1)}, f32[3,32,24,128]{3,2,1,0:T(8,128)}, u32[]{:S(2)}) copy-start(f32[3,32,24,128]{3,2,1,0:T(8,128)} %momentum.3) | copy-start | bytes 3538948
  0.7 6.1 %copy-start.2 = (f32[32,24,128]{2,1,0:T(8,128)S(1)}, f32[32,24,128]{2,1,0:T(8,128)}, u32[]{:S(2)}) copy-start(f32[32,24,128]{2,1,0:T(8,128)} %energy.3) | copy-start | bytes 1179652
  2.3 19.7 %collective-permute-start = (f32[5,3,32,128]{3,2,1,0:T(8,128)S(1)}, f32[5,3,32,128]{3,2,1,0:T(8,128)S(1)}, u32[]{:S(2)}, u32[]{:S(2)}) collective-permute-start(f32[5,3,32,128]{3,2,1,0:T(8,128)S(1)} %get-tuple-element.16), channel_id=1, source_target_pairs={{8,16},{24,0},{16,8},{0,24},{9,17},{25,1},{17,9},{1,25},{10,18},{2... | collective-permute-start | bytes 737288 | tf_op jit(solution)/shard_map/ppermute | solution.py:352
  6.2 15.7 %collective-permute-start.1 = (f32[5,3,32,128]{3,2,1,0:T(8,128)S(1)}, f32[5,3,32,128]{3,2,1,0:T(8,128)S(1)}, u32[]{:S(2)}, u32[]{:S(2)}) collective-permute-start(f32[5,3,32,128]{3,2,1,0:T(8,128)S(1)} %get-tuple-element.17), channel_id=1, source_target_pairs={{0,8},{16,24},{8,0},{24,16},{1,9},{17,25},{9,1},{25,17},{2,10},{18... | collective-permute-start | bytes 737288 | tf_op jit(solution)/shard_map/ppermute | solution.py:352
  13.3 5.9 %collective-permute-start.2 = (f32[5,3,8,128]{3,2,1,0:T(8,128)S(1)}, f32[5,3,8,128]{3,2,1,0:T(8,128)S(1)}, u32[]{:S(2)}, u32[]{:S(2)}) collective-permute-start(f32[5,3,8,128]{3,2,1,0:T(8,128)S(1)} %get-tuple-element.21), channel_id=1, source_target_pairs={{1,2},{3,4},{5,6},{7,0},{2,1},{4,3},{6,5},{0,7},{9,10},{11,12},{13... | collective-permute-start | bytes 184328 | tf_op jit(solution)/shard_map/ppermute | solution.py:352
  15.9 3.4 %collective-permute-start.3 = (f32[5,3,8,128]{3,2,1,0:T(8,128)S(1)}, f32[5,3,8,128]{3,2,1,0:T(8,128)S(1)}, u32[]{:S(2)}, u32[]{:S(2)}) collective-permute-start(f32[5,3,8,128]{3,2,1,0:T(8,128)S(1)} %get-tuple-element.22), channel_id=1, source_target_pairs={{0,1},{2,3},{4,5},{6,7},{1,0},{3,2},{5,4},{7,6},{8,9},{10,11},{12,... | collective-permute-start | bytes 184328 | tf_op jit(solution)/shard_map/ppermute | solution.py:352
  25.0 5.5 %collective-permute-start.4 = (f32[5,3,8,128]{3,2,1,0:T(8,128)S(1)}, f32[5,3,8,128]{3,2,1,0:T(8,128)S(1)}, u32[]{:S(2)}, u32[]{:S(2)}) collective-permute-start(f32[5,3,8,128]{3,2,1,0:T(8,128)S(1)} %get-tuple-element.24), channel_id=1, source_target_pairs={{1,2},{3,4},{5,6},{7,0},{2,1},{4,3},{6,5},{0,7},{9,10},{11,12},{13... | collective-permute-start | bytes 184328 | tf_op jit(solution)/shard_map/ppermute | solution.py:352
  27.1 3.4 %collective-permute-start.5 = (f32[5,3,8,128]{3,2,1,0:T(8,128)S(1)}, f32[5,3,8,128]{3,2,1,0:T(8,128)S(1)}, u32[]{:S(2)}, u32[]{:S(2)}) collective-permute-start(f32[5,3,8,128]{3,2,1,0:T(8,128)S(1)} %get-tuple-element.25), channel_id=1, source_target_pairs={{0,1},{2,3},{4,5},{6,7},{1,0},{3,2},{5,4},{7,6},{8,9},{10,11},{12,... | collective-permute-start | bytes 184328 | tf_op jit(solution)/shard_map/ppermute | solution.py:352
where the time goes:
time: 33.3 us; the launch traced here: 33.2 us
  Pallas kernels  16.5 us (50%)
  starting transfers between devices  9.2 us (28%)
  waiting for transfers between devices  6.71 us (20%)
  between operations  0.71 us (2%)
    pallas_call x4, Pallas kernels, call(): pl.pallas_call(kernel, out_shape=[jax.ShapeDtypeStruct(shape, jnp.float32...  14.9 us
    ppermute x3, starting transfers between devices, exchange(): lax.ppermute(far, axis, pairs[0])  8.66 us
    ppermute x3, waiting for transfers between devices, exchange(): lax.ppermute(far, axis, pairs[0])  6.7 us
    pallas_call x1, Pallas kernels, y_rows(): pl.pallas_call(rows_kernel, out_shape=[pltpu.VMEM(shape, jnp.float32)] *...  1.61 us
  transfers between devices with their start and end apart: 6, of which 2 were waited for; matrix products, arithmetic and copies ran while one was open for 0% of the time, Pallas kernels for 28%

commit v1 on v0

--- a/solution.py
+++ b/solution.py
@@ -185,13 +185,12 @@
                 turned[f, pl.ds(q * count + b, span, stride=quarters * count), :] = block[q * span : (q + 1) * span]
 
 
-def turn_out(turned, count, store):
+def turn_out(turned, count, f, store):
     lanes = turned.shape[-1]
     span = lanes // quarters
-    for f in range(5):
-        for b in range(count):
-            parts = [turned[f, pl.ds(q * count + b, span, stride=quarters * count), :] for q in range(quarters)]
-            store(f, b, jnp.concatenate(parts, axis=0).T)
+    for b in range(count):
+        parts = [turned[f, pl.ds(q * count + b, span, stride=quarters * count), :] for q in range(quarters)]
+        store(f, b, jnp.concatenate(parts, axis=0).T)
 
 
 def ends(turned, count, far, near):
@@ -205,14 +204,13 @@
             near[f, k] = jnp.where(odd, downward, upward)
 
 
-def z_sweep(own, far, near, swept, count):
-    left, right = sides_of("gz", far, near)
+def z_lines(own, count, left=None, right=None):
     width = quarters * count
     span = own.shape[1] // width
     place = lax.broadcasted_iota(jnp.int32, (8, own.shape[-1]), 0)
     for start in range(0, width, 8):
 
-        def load(i):
+        def load(i, start=start):
             if 0 <= i < span:
                 return [own[f, row(i * width + start), :] for f in range(5)]
             if i < 0:
@@ -225,10 +223,29 @@
                 fields = [jnp.where(place >= 8 - count, pltpu.roll(right[f, i - span], 8 - count, 0), a) for f, a in enumerate(fields)]
             return fields
 
-        line = Line(load, 2)
+        yield start, span, Line(load, 2)
+
+
+def z_middle(own, swept, joint, count):
+    for start, span, line in z_lines(own, count):
+        for i in range(halo, span - halo):
+            for f, value in enumerate(line.swept(i)):
+                swept[f, row(i * quarters * count + start), :] = value
+        for end, face in enumerate((halo - 1, span - halo - 1)):
+            for f, value in enumerate(line.flux(face)):
+                joint[f, end, row(start), :] = value
+
+
+def z_ends(own, far, near, middle, joint, swept, count):
+    for start, span, line in z_lines(own, count, *sides_of("gz", far, near)):
+        for end, face in enumerate((halo - 1, span - halo - 1)):
+            line.known[("f", face)] = [joint[f, end, row(start), :] for f in range(5)]
         for i in range(span):
-            for f, value in enumerate(line.swept(i)):
-                swept[f, row(i * width + start), :] = value
+            at = row(i * quarters * count + start)
+            inside = halo <= i < span - halo
+            values = [middle[f, at, :] for f in range(5)] if inside else line.swept(i)
+            for f, value in enumerate(values):
+                swept[f, at, :] = value
 
 
 def inner_kernel(density, momentum, energy, turned, far, near, rim, joint, held, inner):
@@ -302,41 +319,51 @@
     ends(turned, 2, far_end, near_end)
 
 
-def inner_z_kernel(count, own, far, near, out, swept):
+def middle_kernel(count, own, swept, joint):
+    z_middle(own, swept, joint, count)
+
+
+def ends_kernel(count, own, far, near, middle, joint, edges, inner, edges_middle, edges_joint, swept):
     lanes = own.shape[-1]
-    z_sweep(own, far, near, swept, count)
+    z_middle(edges, edges_middle, edges_joint, 2)
+    z_ends(own, far, near, middle, joint, swept, count)
 
     def store(f, b, block):
-        out[f, pl.ds(b * lanes, lanes), :] = block
-
-    turn_out(swept, count, store)
-
-
-def edge_z_kernel(ny, own, far, near, inner, density, momentum, energy, swept):
+        inner[f, pl.ds(b * lanes, lanes), :] = block
+
+    for f in range(5):
+        turn_out(swept, count, f, store)
+
+
+def last_kernel(ny, own, far, near, middle, joint, inner, density, momentum, energy, swept, whole, sent):
     lanes = own.shape[-1]
     nx = density.shape[0] // ny
     deep = lanes // nx
     outs = fields_of(density, momentum, energy)
-    z_sweep(own, far, near, swept, 2)
+    z_ends(own, far, near, middle, joint, swept, 2)
+
+    def store(f, b, block):
+        for r in range(deep):
+            whole[f, pl.ds(b * (ny - deep) + r, nx, stride=ny), :] = block[r * nx : (r + 1) * nx]
+
+    copies = [pltpu.make_async_copy(whole.at[f], outs[f], sent.at[f]) for f in range(5)]
     for f in range(5):
         for i in range(deep, ny - deep):
-            outs[f][pl.ds(i, nx, stride=ny), :] = inner[f, pl.ds((i - deep) * nx, nx), :]
-
-    def store(f, b, block):
-        for r in range(deep):
-            outs[f][pl.ds(b * (ny - deep) + r, nx, stride=ny), :] = block[r * nx : (r + 1) * nx]
-
-    turn_out(swept, 2, store)
-
-
-def call(kernel, shapes, scratch, arguments, in_specs=None):
+            whole[f, pl.ds(i, nx, stride=ny), :] = inner[f, pl.ds((i - deep) * nx, nx), :]
+        turn_out(swept, 2, f, store)
+        copies[f].start()
+    for copy in copies:
+        copy.wait()
+
+
+def call(kernel, shapes, scratch, arguments, in_specs=None, out_spec=None):
     whole = pl.BlockSpec(memory_space=pltpu.VMEM)
     return pl.pallas_call(
         kernel,
         out_shape=[jax.ShapeDtypeStruct(shape, jnp.float32) for shape in shapes],
         in_specs=[whole] * len(arguments) if in_specs is None else in_specs,
-        out_specs=[whole] * len(shapes),
-        scratch_shapes=[pltpu.VMEM(shape, jnp.float32) for shape in scratch],
+        out_specs=[whole if out_spec is None else out_spec] * len(shapes),
+        scratch_shapes=[pltpu.VMEM(a, jnp.float32) if isinstance(a, tuple) else a for a in scratch],
         compiler_params=pltpu.CompilerParams(vmem_limit_bytes=24 * 2**20),
     )(*arguments)
 
@@ -380,27 +407,34 @@
         [density, momentum, energy],
     )
     far, near = exchange("gz", far, near)
-    (inner,) = call(
-        functools.partial(inner_z_kernel, count),
-        [(5, count * nz, nz)],
-        [(5, count * nz, nz)],
-        [turned, far, near],
-    )
-    whole = pl.BlockSpec(memory_space=pltpu.VMEM)
-    turned, far, near = call(
+    middle, faces = call(
+        functools.partial(middle_kernel, count),
+        [(5, count * nz, nz), (5, 2, quarters * count, nz)],
+        [],
+        [turned],
+    )
+    whole, anywhere = (pl.BlockSpec(memory_space=space) for space in (pltpu.VMEM, pl.ANY))
+    edges, far_edges, near_edges = call(
         edge_kernel,
         [(5, 2 * nz, nz), end, end],
         [(5, 2 * halo, nx, nz), (5, 2 * nz, nz)],
-        [far_rows, near_rows, rim, joint, inner],
-        [whole] * 4 + [pl.BlockSpec(memory_space=pl.ANY)],
-    )
-    far, near = exchange("gz", far, near)
+        [far_rows, near_rows, rim, joint, faces],
+        [whole] * 4 + [anywhere],
+    )
+    far_edges, near_edges = exchange("gz", far_edges, near_edges)
+    inner, edges_middle, edges_faces = call(
+        functools.partial(ends_kernel, count),
+        [(5, count * nz, nz), (5, 2 * nz, nz), (5, 2, quarters * 2, nz)],
+        [(5, count * nz, nz)],
+        [turned, far, near, middle, faces, edges],
+    )
     cells = nx * ny
     outs = call(
-        functools.partial(edge_z_kernel, ny),
+        functools.partial(last_kernel, ny),
         [(cells, nz), (3, cells, nz), (cells, nz)],
-        [(5, 2 * nz, nz)],
-        [turned, far, near, inner],
+        [(5, 2 * nz, nz), (5, cells, nz), pltpu.SemaphoreType.DMA((5,))],
+        [edges, far_edges, near_edges, edges_middle, edges_faces, inner],
+        out_spec=anywhere,
     )
     return (outs[0].reshape(nx, ny, nz), outs[1].reshape(3, nx, ny, nz), outs[2].reshape(nx, ny, nz))
 

time: 33.3 us -> 28.5 us (0.86)
  waiting for transfers between devices: 6.71 us -> 1.84 us
    ppermute x3, waiting for transfers between devices: 6.7 us -> 1.81 us  [exchange(): lax.ppermute(far, axis, pairs[0])]
    pallas_call x4 -> x5, Pallas kernels: 14.9 us -> 14.9 us  [call(): pl.pallas_call(kernel, out_shape=[jax.ShapeDtypeStruct(shape, jnp.float32...]
  transfers between devices with their start and end apart: 6 -> 6, of which waited for: 2 -> 1; matrix products, arithmetic and copies ran while one was open for 0% -> 0% of each run, Pallas kernels for 28% -> 47%
where the time goes in v1:
time: 28.5 us; the launch traced here: 28.3 us
  Pallas kernels  16.5 us (58%)
  starting transfers between devices  9.27 us (33%)
  waiting for transfers between devices  1.84 us (6%)
  between operations  0.7 us (2%)
    pallas_call x5, Pallas kernels, call(): pl.pallas_call(kernel, out_shape=[jax.ShapeDtypeStruct(shape, jnp.float32...  14.9 us
    ppermute x3, starting transfers between devices, exchange(): lax.ppermute(far, axis, pairs[0])  8.73 us
    ppermute x3, waiting for transfers between devices, exchange(): lax.ppermute(far, axis, pairs[0])  1.81 us
    pallas_call x1, Pallas kernels, y_rows(): pl.pallas_call(rows_kernel, out_shape=[pltpu.VMEM(shape, jnp.float32)] *...  1.61 us
  transfers between devices with their start and end apart: 6, of which 1 were waited for; matrix products, arithmetic and copies ran while one was open for 0% of the time, Pallas kernels for 47%

profile of v1, /device:TPU:0, one launch (start us, length us, event | category | flops | bytes accessed | tf_op | source)
XLA Modules:
  0.0 28.3 jit_solution(11639330973501614648)
XLA Ops:
  0.6 0.0 copy-start.1
  0.6 0.0 copy-start
  0.7 0.0 copy-start.2
  0.7 1.6 %shard_map.58 = (f32[5,3,32,128]{3,2,1,0:T(8,128)S(1)}, f32[5,3,32,128]{3,2,1,0:T(8,128)S(1)}) custom-call(f32[32,24,128]{2,1,0:T(8,128)} %density.3, f32[3,32,24,128]{3,2,1,0:T(8,128)} %momentum.3, f32[32,24,128]{2,1,0:T(8,128)} %energy.3), custom_call_target="tpu_custom_call" | custom-call | tf_op jit(solution)/shard_map/pallas_call | solution.py:385
  2.3 4.0 %collective-permute-start = (f32[5,3,32,128]{3,2,1,0:T(8,128)S(1)}, f32[5,3,32,128]{3,2,1,0:T(8,128)S(1)}, u32[]{:S(2)}, u32[]{:S(2)}) collective-permute-start(f32[5,3,32,128]{3,2,1,0:T(8,128)S(1)} %get-tuple-element.21), channel_id=1, source_target_pairs={{8,16},{24,0},{16,8},{0,24},{9,17},{25,1},{17,9},{1,25},{10,18},{2... | collective-permute-start | bytes 737288 | tf_op jit(solution)/shard_map/ppermute | solution.py:379
  6.2 0.5 %collective-permute-start.1 = (f32[5,3,32,128]{3,2,1,0:T(8,128)S(1)}, f32[5,3,32,128]{3,2,1,0:T(8,128)S(1)}, u32[]{:S(2)}, u32[]{:S(2)}) collective-permute-start(f32[5,3,32,128]{3,2,1,0:T(8,128)S(1)} %get-tuple-element.22), channel_id=1, source_target_pairs={{0,8},{16,24},{8,0},{24,16},{1,9},{17,25},{9,1},{25,17},{2,10},{18... | collective-permute-start | bytes 737288 | tf_op jit(solution)/shard_map/ppermute | solution.py:379
  6.8 0.0 copy-done.1
  6.8 0.0 copy-done
  6.8 0.0 copy-done.2
  6.8 6.5 %shard_map.59 = (f32[5,512,128]{2,1,0:T(8,128)S(1)}, f32[5,3,8,128]{3,2,1,0:T(8,128)S(1)}, f32[5,3,8,128]{3,2,1,0:T(8,128)S(1)}, f32[5,12,32,128]{3,2,1,0:T(8,128)S(1)}, f32[5,2,32,128]{3,2,1,0:T(8,128)S(1)}) custom-call(f32[32,24,128]{2,1,0:T(8,128)S(1)} %copy-done.1, f32[3,32,24,128]{3,2,1,0:T(8,128)S(1)} %copy-done, f32[32,24,128]{2,1,0:T(8,128)S(1)} %copy-done.2), custom_call_target="tpu_custom_call" | custom-call | tf_op jit(solution)/shard_map/pallas_call | solution.py:361
  13.3 2.5 %collective-permute-start.4 = (f32[5,3,8,128]{3,2,1,0:T(8,128)S(1)}, f32[5,3,8,128]{3,2,1,0:T(8,128)S(1)}, u32[]{:S(2)}, u32[]{:S(2)}) collective-permute-start(f32[5,3,8,128]{3,2,1,0:T(8,128)S(1)} %get-tuple-element.30), channel_id=1, source_target_pairs={{1,2},{3,4},{5,6},{7,0},{2,1},{4,3},{6,5},{0,7},{9,10},{11,12},{13... | collective-permute-start | bytes 184328 | tf_op jit(solution)/shard_map/ppermute | solution.py:379
  15.9 0.0 collective-permute-start.5
  15.9 1.8 %shard_map.60 = (f32[5,512,128]{2,1,0:T(8,128)S(1)}, f32[5,2,16,128]{3,2,1,0:T(8,128)S(1)}) custom-call(f32[5,512,128]{2,1,0:T(8,128)S(1)} %get-tuple-element.25.own), custom_call_target="tpu_custom_call" | custom-call | tf_op jit(solution)/shard_map/pallas_call | solution.py:361
  17.7 0.0 collective-permute-done.far
  17.7 0.0 collective-permute-done.1.near
  17.7 3.0 %shard_map.61 = (f32[5,256,128]{2,1,0:T(8,128)S(1)}, f32[5,3,8,128]{3,2,1,0:T(8,128)S(1)}, f32[5,3,8,128]{3,2,1,0:T(8,128)S(1)}) custom-call(f32[5,3,32,128]{3,2,1,0:T(8,128)S(1)} %collective-permute-done.far, f32[5,3,32,128]{3,2,1,0:T(8,128)S(1)} %collective-permute-done.1.near, f32[5,12,32,128]{3,2,1,0:T(8,128)S(1)} %get-tuple-element.23.rim, ...), custom_call_target="tpu_custom_call" | custom-call | tf_op jit(solution)/shard_map/pallas_call | solution.py:361
  20.7 2.2 %collective-permute-start.2 = (f32[5,3,8,128]{3,2,1,0:T(8,128)S(1)}, f32[5,3,8,128]{3,2,1,0:T(8,128)S(1)}, u32[]{:S(2)}, u32[]{:S(2)}) collective-permute-start(f32[5,3,8,128]{3,2,1,0:T(8,128)S(1)} %get-tuple-element.28), channel_id=1, source_target_pairs={{1,2},{3,4},{5,6},{7,0},{2,1},{4,3},{6,5},{0,7},{9,10},{11,12},{13... | collective-permute-start | bytes 184328 | tf_op jit(solution)/shard_map/ppermute | solution.py:379
  22.9 0.0 collective-permute-start.3
  22.9 0.0 collective-permute-done.4.far
  22.9 0.0 collective-permute-done.5.near
  22.9 1.9 %shard_map.62 = (f32[5,512,128]{2,1,0:T(8,128)S(1)}, f32[5,256,128]{2,1,0:T(8,128)S(1)}, f32[5,2,8,128]{3,2,1,0:T(8,128)S(1)}) custom-call(f32[5,512,128]{2,1,0:T(8,128)S(1)} %get-tuple-element.25.own, f32[5,3,8,128]{3,2,1,0:T(8,128)S(1)} %collective-permute-done.4.far, f32[5,3,8,128]{3,2,1,0:T(8,128)S(1)} %collective-permute-done.5.near, ...), custom_call_target="tpu_custom_call" | custom-call | tf_op jit(solution)/shard_map/pallas_call | solution.py:361
  24.8 1.8 %collective-permute-done.2.far = f32[5,3,8,128]{3,2,1,0:T(8,128)S(1)} collective-permute-done((f32[5,3,8,128]{3,2,1,0:T(8,128)S(1)}, f32[5,3,8,128]{3,2,1,0:T(8,128)S(1)}, u32[]{:S(2)}, u32[]{:S(2)}) %collective-permute-start.2) | collective-permute-done | bytes 61472 | tf_op jit(solution)/shard_map/ppermute | solution.py:379
  26.6 0.0 collective-permute-done.3.near
  26.6 1.7 %shard_map.63 = (f32[768,128]{1,0:T(8,128)}, f32[3,768,128]{2,1,0:T(8,128)}, f32[768,128]{1,0:T(8,128)}) custom-call(f32[5,256,128]{2,1,0:T(8,128)S(1)} %get-tuple-element.27.edges.own, f32[5,3,8,128]{3,2,1,0:T(8,128)S(1)} %collective-permute-done.2.far, f32[5,3,8,128]{3,2,1,0:T(8,128)S(1)} %collective-permute-done.3.near, ...), custom_call_target="tpu_custom_call" | custom-call | tf_op jit(solution)/shard_map/pallas_call | solution.py:361
Async XLA Ops:
  0.6 6.1 %copy-start.1 = (f32[32,24,128]{2,1,0:T(8,128)S(1)}, f32[32,24,128]{2,1,0:T(8,128)}, u32[]{:S(2)}) copy-start(f32[32,24,128]{2,1,0:T(8,128)} %density.3) | copy-start | bytes 1179652
  0.6 6.1 %copy-start = (f32[3,32,24,128]{3,2,1,0:T(8,128)S(1)}, f32[3,32,24,128]{3,2,1,0:T(8,128)}, u32[]{:S(2)}) copy-start(f32[3,32,24,128]{3,2,1,0:T(8,128)} %momentum.3) | copy-start | bytes 3538948
  0.7 6.1 %copy-start.2 = (f32[32,24,128]{2,1,0:T(8,128)S(1)}, f32[32,24,128]{2,1,0:T(8,128)}, u32[]{:S(2)}) copy-start(f32[32,24,128]{2,1,0:T(8,128)} %energy.3) | copy-start | bytes 1179652
  2.3 15.4 %collective-permute-start = (f32[5,3,32,128]{3,2,1,0:T(8,128)S(1)}, f32[5,3,32,128]{3,2,1,0:T(8,128)S(1)}, u32[]{:S(2)}, u32[]{:S(2)}) collective-permute-start(f32[5,3,32,128]{3,2,1,0:T(8,128)S(1)} %get-tuple-element.21), channel_id=1, source_target_pairs={{8,16},{24,0},{16,8},{0,24},{9,17},{25,1},{17,9},{1,25},{10,18},{2... | collective-permute-start | bytes 737288 | tf_op jit(solution)/shard_map/ppermute | solution.py:379
  6.2 11.5 %collective-permute-start.1 = (f32[5,3,32,128]{3,2,1,0:T(8,128)S(1)}, f32[5,3,32,128]{3,2,1,0:T(8,128)S(1)}, u32[]{:S(2)}, u32[]{:S(2)}) collective-permute-start(f32[5,3,32,128]{3,2,1,0:T(8,128)S(1)} %get-tuple-element.22), channel_id=1, source_target_pairs={{0,8},{16,24},{8,0},{24,16},{1,9},{17,25},{9,1},{25,17},{2,10},{18... | collective-permute-start | bytes 737288 | tf_op jit(solution)/shard_map/ppermute | solution.py:379
  13.3 9.6 %collective-permute-start.4 = (f32[5,3,8,128]{3,2,1,0:T(8,128)S(1)}, f32[5,3,8,128]{3,2,1,0:T(8,128)S(1)}, u32[]{:S(2)}, u32[]{:S(2)}) collective-permute-start(f32[5,3,8,128]{3,2,1,0:T(8,128)S(1)} %get-tuple-element.30), channel_id=1, source_target_pairs={{1,2},{3,4},{5,6},{7,0},{2,1},{4,3},{6,5},{0,7},{9,10},{11,12},{13... | collective-permute-start | bytes 184328 | tf_op jit(solution)/shard_map/ppermute | solution.py:379
  15.9 7.1 %collective-permute-start.5 = (f32[5,3,8,128]{3,2,1,0:T(8,128)S(1)}, f32[5,3,8,128]{3,2,1,0:T(8,128)S(1)}, u32[]{:S(2)}, u32[]{:S(2)}) collective-permute-start(f32[5,3,8,128]{3,2,1,0:T(8,128)S(1)} %get-tuple-element.31), channel_id=1, source_target_pairs={{0,1},{2,3},{4,5},{6,7},{1,0},{3,2},{5,4},{7,6},{8,9},{10,11},{12,... | collective-permute-start | bytes 184328 | tf_op jit(solution)/shard_map/ppermute | solution.py:379
  20.7 5.9 %collective-permute-start.2 = (f32[5,3,8,128]{3,2,1,0:T(8,128)S(1)}, f32[5,3,8,128]{3,2,1,0:T(8,128)S(1)}, u32[]{:S(2)}, u32[]{:S(2)}) collective-permute-start(f32[5,3,8,128]{3,2,1,0:T(8,128)S(1)} %get-tuple-element.28), channel_id=1, source_target_pairs={{1,2},{3,4},{5,6},{7,0},{2,1},{4,3},{6,5},{0,7},{9,10},{11,12},{13... | collective-permute-start | bytes 184328 | tf_op jit(solution)/shard_map/ppermute | solution.py:379
  22.9 3.7 %collective-permute-start.3 = (f32[5,3,8,128]{3,2,1,0:T(8,128)S(1)}, f32[5,3,8,128]{3,2,1,0:T(8,128)S(1)}, u32[]{:S(2)}, u32[]{:S(2)}) collective-permute-start(f32[5,3,8,128]{3,2,1,0:T(8,128)S(1)} %get-tuple-element.29), channel_id=1, source_target_pairs={{0,1},{2,3},{4,5},{6,7},{1,0},{3,2},{5,4},{7,6},{8,9},{10,11},{12,... | collective-permute-start | bytes 184328 | tf_op jit(solution)/shard_map/ppermute | solution.py:379

commit v2 on v1

--- a/solution.py
+++ b/solution.py
@@ -22,15 +22,19 @@
     return [density, vx, vy, vz, pressure]
 
 
+def signed(step):
+    return step, jnp.maximum(step, 0.0), jnp.minimum(step, 0.0)
+
+
 def half_slope(ahead, behind):
-    top = jnp.maximum(jnp.minimum(ahead, behind), 0.0)
-    bottom = jnp.minimum(jnp.maximum(ahead, behind), 0.0)
-    return jnp.maximum(jnp.minimum(0.25 * (ahead + behind), top), bottom)
+    top = jnp.minimum(ahead[1], behind[1])
+    bottom = jnp.maximum(ahead[2], behind[2])
+    return jnp.maximum(jnp.minimum(0.25 * (ahead[0] + behind[0]), top), bottom)
 
 
 def face_offset(ahead, slope, slope_next):
-    offset = 0.5 * ahead - (1.0 / 3.0) * (slope_next - slope)
-    return jnp.minimum(jnp.maximum(offset, jnp.minimum(ahead, 0.0)), jnp.maximum(ahead, 0.0))
+    offset = 0.5 * ahead[0] - (1.0 / 3.0) * (slope_next - slope)
+    return jnp.minimum(jnp.maximum(offset, ahead[2]), ahead[1])
 
 
 def limited(first, second):
@@ -84,7 +88,7 @@
         return self.once("q", i, lambda i: primitives(self.load(i)))
 
     def diff(self, i):
-        return self.once("d", i, lambda i: [b - a for a, b in zip(self.prims(i), self.prims(i + 1))])
+        return self.once("d", i, lambda i: [signed(b - a) for a, b in zip(self.prims(i), self.prims(i + 1))])
 
     def slope(self, i):
         return self.once("s", i, lambda i: [half_slope(a, b) for a, b in zip(self.diff(i), self.diff(i - 1))])
@@ -93,7 +97,7 @@
         return self.once("u", i, lambda i: [face_offset(d, s, t) for d, s, t in zip(self.diff(i), self.slope(i), self.slope(i + 1))])
 
     def down(self, i):
-        return self.once("w", i, lambda i: [d - u for d, u in zip(self.diff(i - 1), self.up(i - 1))])
+        return self.once("w", i, lambda i: [d[0] - u for d, u in zip(self.diff(i - 1), self.up(i - 1))])
 
     def low(self, i):
         return self.once("l", i, lambda i: [q - limited(w, u) for q, w, u in zip(self.prims(i), self.down(i), self.up(i))])
@@ -114,8 +118,8 @@
     low, high = [], []
     for q in states:
         d = ahead(q) - q
-        s = half_slope(d, behind(d))
-        u = face_offset(d, s, ahead(s))
+        s = half_slope(signed(d), signed(behind(d)))
+        u = face_offset(signed(d), s, ahead(s))
         w = behind(d - u)
         low.append(ahead(q - limited(w, u)))
         high.append(q + limited(u, w))
@@ -173,16 +177,24 @@
             near[f, r] = jnp.where(odd, first, last)
 
 
-def turn_in(source, turned, count):
+def alternate(steps, parts, others, other_parts):
+    made = 0
+    for part, _ in enumerate(steps):
+        while made * parts < (part + 1) * other_parts:
+            next(others, None)
+            made += 1
+    for _ in others:
+        pass
+
+
+def turn_in(source, turned, count, b):
     lanes = source.shape[-1]
     span = lanes // quarters
-
-    @pl.loop(0, 5)
-    def _(f):
-        for b in range(count):
-            block = source[f, pl.ds(b * lanes, lanes), :].T
-            for q in range(quarters):
-                turned[f, pl.ds(q * count + b, span, stride=quarters * count), :] = block[q * span : (q + 1) * span]
+    for f in range(5):
+        block = source[f].T
+        for q in range(quarters):
+            turned[f, pl.ds(q * count + b, span, stride=quarters * count), :] = block[q * span : (q + 1) * span]
+        yield
 
 
 def turn_out(turned, count, f, store):
@@ -191,6 +203,7 @@
     for b in range(count):
         parts = [turned[f, pl.ds(q * count + b, span, stride=quarters * count), :] for q in range(quarters)]
         store(f, b, jnp.concatenate(parts, axis=0).T)
+        yield
 
 
 def ends(turned, count, far, near):
@@ -231,6 +244,7 @@
         for i in range(halo, span - halo):
             for f, value in enumerate(line.swept(i)):
                 swept[f, row(i * quarters * count + start), :] = value
+            yield
         for end, face in enumerate((halo - 1, span - halo - 1)):
             for f, value in enumerate(line.flux(face)):
                 joint[f, end, row(start), :] = value
@@ -248,7 +262,7 @@
                 swept[f, at, :] = value
 
 
-def inner_kernel(density, momentum, energy, turned, far, near, rim, joint, held, inner):
+def inner_kernel(density, momentum, energy, turned, far, near, rim, joint, held, *strips):
     nx, ny, lanes = density.shape
     deep = lanes // nx
     sources = fields_of(density, momentum, energy)
@@ -261,13 +275,13 @@
             for f, value in enumerate(line.swept(i)):
                 held[f, pl.ds(pl.multiple_of(i * ny + start, 8), 8), :] = value
 
-    @pl.loop(0, nx // 8)
-    def _(tile):
-        some = pl.ds(pl.multiple_of(tile * 8, 8), 8)
+    def sweep(tile):
+        some = row(tile * 8)
         line = Line(lambda i: [held[f, pl.ds(tile * (8 * ny) + i, 8, stride=ny), :] for f in range(5)], 1)
         for i in range(deep, ny - deep):
             for f, value in enumerate(line.swept(i)):
-                inner[f, pl.ds(pl.multiple_of((i - deep) * nx + tile * 8, 8), 8), :] = value
+                strips[tile][f, row((i - deep) * 8), :] = value
+            yield
         for f in range(5):
             joint[f, 0, some, :] = line.flux(deep - 1)[f]
             joint[f, 1, some, :] = line.flux(ny - deep - 1)[f]
@@ -277,12 +291,17 @@
                 rim[f, r, some, :] = a
                 rim[f, kept + r, some, :] = b
 
-    count = ny // deep - 2
-    turn_in(inner, turned, count)
+    count = len(strips)
+    turns = iter(())
+    for tile in range(count):
+        alternate(sweep(tile), ny - 2 * deep, turns, 5)
+        turns = turn_in(strips[tile], turned, count, tile)
+    for _ in turns:
+        pass
     ends(turned, count, far, near)
 
 
-def edge_kernel(far, near, rim, joint, _, turned, far_end, near_end, ghost, outer):
+def edge_kernel(far, near, rim, joint, _, turned, far_end, near_end, ghost, *outers):
     _, kept, nx, lanes = rim.shape
     kept = kept // 2
     deep = lanes // nx
@@ -296,61 +315,76 @@
             for f in range(5):
                 ghost[f, side * halo + r] = fields[f] - (flux[f] - behind(flux[f]))
 
-    @pl.loop(0, nx // 8)
-    def _(tile):
-        some = pl.ds(pl.multiple_of(tile * 8, 8), 8)
-        for side in range(2):
-
-            def load(i):
-                if side == 0:
-                    source, at = (ghost, i + halo) if i < 0 else (rim, i)
-                else:
-                    source, at = (ghost, i - deep + halo) if i >= deep else (rim, i + kept + kept - deep)
-                return [source[f, at, some, :] for f in range(5)]
-
-            line = Line(load, 1)
-            known = deep - 1 if side == 0 else -1
-            line.known[("f", known)] = [joint[f, side, some, :] for f in range(5)]
-            for i in range(deep):
-                for f, value in enumerate(line.swept(i)):
-                    outer[f, pl.ds(pl.multiple_of((side * deep + i) * nx + tile * 8, 8), 8), :] = value
-
-    turn_in(outer, turned, 2)
+    share = nx // 8 // len(outers)
+
+    def sweep(block):
+        for half in range(share):
+            some = row((block * share + half) * 8)
+            for side in range(2):
+
+                def load(i, side=side, some=some):
+                    if side == 0:
+                        source, at = (ghost, i + halo) if i < 0 else (rim, i)
+                    else:
+                        source, at = (ghost, i - deep + halo) if i >= deep else (rim, i + kept + kept - deep)
+                    return [source[f, at, some, :] for f in range(5)]
+
+                line = Line(load, 1)
+                known = deep - 1 if side == 0 else -1
+                line.known[("f", known)] = [joint[f, side, some, :] for f in range(5)]
+                for i in range(deep):
+                    for f, value in enumerate(line.swept(i)):
+                        outers[block][f, row(((half * 2 + side) * deep + i) * 8), :] = value
+                    yield
+
+    turns = iter(())
+    for block, outer in enumerate(outers):
+        alternate(sweep(block), share * 2 * deep, turns, 5)
+        turns = turn_in(outer, turned, len(outers), block)
+    for _ in turns:
+        pass
     ends(turned, 2, far_end, near_end)
 
 
 def middle_kernel(count, own, swept, joint):
-    z_middle(own, swept, joint, count)
+    for _ in z_middle(own, swept, joint, count):
+        pass
 
 
 def ends_kernel(count, own, far, near, middle, joint, edges, inner, edges_middle, edges_joint, swept):
     lanes = own.shape[-1]
-    z_middle(edges, edges_middle, edges_joint, 2)
     z_ends(own, far, near, middle, joint, swept, count)
 
     def store(f, b, block):
         inner[f, pl.ds(b * lanes, lanes), :] = block
 
-    for f in range(5):
-        turn_out(swept, count, f, store)
+    cells = edges.shape[1] // (quarters * 2) - 2 * halo
+    turns = (None for f in range(5) for _ in turn_out(swept, count, f, store))
+    alternate(z_middle(edges, edges_middle, edges_joint, 2), cells, turns, 5 * count)
 
 
 def last_kernel(ny, own, far, near, middle, joint, inner, density, momentum, energy, swept, whole, sent):
     lanes = own.shape[-1]
     nx = density.shape[0] // ny
     deep = lanes // nx
+    strip = 2 * deep * 8
     outs = fields_of(density, momentum, energy)
     z_ends(own, far, near, middle, joint, swept, 2)
 
     def store(f, b, block):
-        for r in range(deep):
-            whole[f, pl.ds(b * (ny - deep) + r, nx, stride=ny), :] = block[r * nx : (r + 1) * nx]
+        for half in range(lanes // strip):
+            for k in range(2 * deep):
+                y = k if k < deep else ny - 2 * deep + k
+                at = half * strip + k * 8
+                whole[f, pl.ds((b * (lanes // strip) + half) * 8 * ny + y, 8, stride=ny), :] = block[at : at + 8]
 
     copies = [pltpu.make_async_copy(whole.at[f], outs[f], sent.at[f]) for f in range(5)]
     for f in range(5):
-        for i in range(deep, ny - deep):
-            whole[f, pl.ds(i, nx, stride=ny), :] = inner[f, pl.ds((i - deep) * nx, nx), :]
-        turn_out(swept, 2, f, store)
+        for b in range(nx // 8):
+            for i in range(deep, ny - deep):
+                whole[f, pl.ds(b * 8 * ny + i, 8, stride=ny), :] = inner[f, row(b * lanes + (i - deep) * 8), :]
+        for _ in turn_out(swept, 2, f, store):
+            pass
         copies[f].start()
     for copy in copies:
         copy.wait()
@@ -403,7 +437,7 @@
     turned, far, near, rim, joint = call(
         inner_kernel,
         [(5, count * nz, nz), end, end, (5, 2 * kept, nx, nz), (5, 2, nx, nz)],
-        [(5, nx * ny, nz), (5, count * nz, nz)],
+        [(5, nx * ny, nz)] + [(5, nz, nz)] * count,
         [density, momentum, energy],
     )
     far, near = exchange("gz", far, near)
@@ -417,7 +451,7 @@
     edges, far_edges, near_edges = call(
         edge_kernel,
         [(5, 2 * nz, nz), end, end],
-        [(5, 2 * halo, nx, nz), (5, 2 * nz, nz)],
+        [(5, 2 * halo, nx, nz)] + [(5, nz, nz)] * 2,
         [far_rows, near_rows, rim, joint, faces],
         [whole] * 4 + [anywhere],
     )

time: 28.5 us -> 27.9 us (0.979)
  Pallas kernels: 16.5 us -> 15 us
  waiting for transfers between devices: 1.84 us -> 2.75 us
    pallas_call x5, Pallas kernels: 14.9 us -> 13.4 us  [call(): pl.pallas_call(kernel, out_shape=[jax.ShapeDtypeStruct(shape, jnp.float32...]
    ppermute x3, waiting for transfers between devices: 0.03 us -> 0.89 us  [exchange(): lax.ppermute(near, axis, pairs[1])]
  transfers between devices with their start and end apart: 6 -> 6, of which waited for: 1 -> 2; matrix products, arithmetic and copies ran while one was open for 0% -> 0% of each run, Pallas kernels for 47% -> 42%
where the time goes in v2:
time: 27.9 us; the launch traced here: 27.8 us
  Pallas kernels  15 us (54%)
  starting transfers between devices  9.28 us (33%)
  waiting for transfers between devices  2.75 us (10%)
  between operations  0.7 us (3%)
    pallas_call x5, Pallas kernels, call(): pl.pallas_call(kernel, out_shape=[jax.ShapeDtypeStruct(shape, jnp.float32...  13.4 us
    ppermute x3, starting transfers between devices, exchange(): lax.ppermute(far, axis, pairs[0])  8.74 us
    ppermute x3, waiting for transfers between devices, exchange(): lax.ppermute(far, axis, pairs[0])  1.86 us
    pallas_call x1, Pallas kernels, y_rows(): pl.pallas_call(rows_kernel, out_shape=[pltpu.VMEM(shape, jnp.float32)] *...  1.61 us
    ppermute x3, waiting for transfers between devices, exchange(): lax.ppermute(near, axis, pairs[1])  0.89 us
  transfers between devices with their start and end apart: 6, of which 2 were waited for; matrix products, arithmetic and copies ran while one was open for 0% of the time, Pallas kernels for 42%

profile of v2, /device:TPU:0, one launch (start us, length us, event | category | flops | bytes accessed | tf_op | source)
XLA Modules:
  0.0 27.8 jit_solution(708969162145134764)
XLA Ops:
  0.6 0.0 copy-start.1
  0.6 0.0 copy-start
  0.7 0.0 copy-start.2
  0.7 1.6 %shard_map.58 = (f32[5,3,32,128]{3,2,1,0:T(8,128)S(1)}, f32[5,3,32,128]{3,2,1,0:T(8,128)S(1)}) custom-call(f32[32,24,128]{2,1,0:T(8,128)} %density.3, f32[3,32,24,128]{3,2,1,0:T(8,128)} %momentum.3, f32[32,24,128]{2,1,0:T(8,128)} %energy.3), custom_call_target="tpu_custom_call" | custom-call | tf_op jit(solution)/shard_map/pallas_call | solution.py:419
  2.3 4.0 %collective-permute-start = (f32[5,3,32,128]{3,2,1,0:T(8,128)S(1)}, f32[5,3,32,128]{3,2,1,0:T(8,128)S(1)}, u32[]{:S(2)}, u32[]{:S(2)}) collective-permute-start(f32[5,3,32,128]{3,2,1,0:T(8,128)S(1)} %get-tuple-element.21), channel_id=1, source_target_pairs={{8,16},{24,0},{16,8},{0,24},{9,17},{25,1},{17,9},{1,25},{10,18},{2... | collective-permute-start | bytes 737288 | tf_op jit(solution)/shard_map/ppermute | solution.py:413
  6.2 0.5 %collective-permute-start.1 = (f32[5,3,32,128]{3,2,1,0:T(8,128)S(1)}, f32[5,3,32,128]{3,2,1,0:T(8,128)S(1)}, u32[]{:S(2)}, u32[]{:S(2)}) collective-permute-start(f32[5,3,32,128]{3,2,1,0:T(8,128)S(1)} %get-tuple-element.22), channel_id=1, source_target_pairs={{0,8},{16,24},{8,0},{24,16},{1,9},{17,25},{9,1},{25,17},{2,10},{18... | collective-permute-start | bytes 737288 | tf_op jit(solution)/shard_map/ppermute | solution.py:413
  6.8 0.0 copy-done.1
  6.8 0.0 copy-done
  6.8 0.0 copy-done.2
  6.8 5.7 %shard_map.59 = (f32[5,512,128]{2,1,0:T(8,128)S(1)}, f32[5,3,8,128]{3,2,1,0:T(8,128)S(1)}, f32[5,3,8,128]{3,2,1,0:T(8,128)S(1)}, f32[5,12,32,128]{3,2,1,0:T(8,128)S(1)}, f32[5,2,32,128]{3,2,1,0:T(8,128)S(1)}) custom-call(f32[32,24,128]{2,1,0:T(8,128)S(1)} %copy-done.1, f32[3,32,24,128]{3,2,1,0:T(8,128)S(1)} %copy-done, f32[32,24,128]{2,1,0:T(8,128)S(1)} %copy-done.2), custom_call_target="tpu_custom_call" | custom-call | tf_op jit(solution)/shard_map/pallas_call | solution.py:395
  12.5 2.5 %collective-permute-start.4 = (f32[5,3,8,128]{3,2,1,0:T(8,128)S(1)}, f32[5,3,8,128]{3,2,1,0:T(8,128)S(1)}, u32[]{:S(2)}, u32[]{:S(2)}) collective-permute-start(f32[5,3,8,128]{3,2,1,0:T(8,128)S(1)} %get-tuple-element.30), channel_id=1, source_target_pairs={{1,2},{3,4},{5,6},{7,0},{2,1},{4,3},{6,5},{0,7},{9,10},{11,12},{13... | collective-permute-start | bytes 184328 | tf_op jit(solution)/shard_map/ppermute | solution.py:413
  15.1 0.0 collective-permute-start.5
  15.1 1.7 %shard_map.60 = (f32[5,512,128]{2,1,0:T(8,128)S(1)}, f32[5,2,16,128]{3,2,1,0:T(8,128)S(1)}) custom-call(f32[5,512,128]{2,1,0:T(8,128)S(1)} %get-tuple-element.25.own), custom_call_target="tpu_custom_call" | custom-call | tf_op jit(solution)/shard_map/pallas_call | solution.py:395
  16.8 0.0 collective-permute-done.far
  16.8 0.9 %collective-permute-done.1.near = f32[5,3,32,128]{3,2,1,0:T(8,128)S(1)} collective-permute-done((f32[5,3,32,128]{3,2,1,0:T(8,128)S(1)}, f32[5,3,32,128]{3,2,1,0:T(8,128)S(1)}, u32[]{:S(2)}, u32[]{:S(2)}) %collective-permute-start.1) | collective-permute-done | bytes 245792 | tf_op jit(solution)/shard_map/ppermute | solution.py:413
  17.7 2.4 %shard_map.61 = (f32[5,256,128]{2,1,0:T(8,128)S(1)}, f32[5,3,8,128]{3,2,1,0:T(8,128)S(1)}, f32[5,3,8,128]{3,2,1,0:T(8,128)S(1)}) custom-call(f32[5,3,32,128]{3,2,1,0:T(8,128)S(1)} %collective-permute-done.far, f32[5,3,32,128]{3,2,1,0:T(8,128)S(1)} %collective-permute-done.1.near, f32[5,12,32,128]{3,2,1,0:T(8,128)S(1)} %get-tuple-element.23.rim, ...), custom_call_target="tpu_custom_call" | custom-call | tf_op jit(solution)/shard_map/pallas_call | solution.py:395
  20.2 2.2 %collective-permute-start.2 = (f32[5,3,8,128]{3,2,1,0:T(8,128)S(1)}, f32[5,3,8,128]{3,2,1,0:T(8,128)S(1)}, u32[]{:S(2)}, u32[]{:S(2)}) collective-permute-start(f32[5,3,8,128]{3,2,1,0:T(8,128)S(1)} %get-tuple-element.28), channel_id=1, source_target_pairs={{1,2},{3,4},{5,6},{7,0},{2,1},{4,3},{6,5},{0,7},{9,10},{11,12},{13... | collective-permute-start | bytes 184328 | tf_op jit(solution)/shard_map/ppermute | solution.py:413
  22.4 0.0 collective-permute-start.3
  22.4 0.0 collective-permute-done.4.far
  22.4 0.0 collective-permute-done.5.near
  22.4 1.8 %shard_map.62 = (f32[5,512,128]{2,1,0:T(8,128)S(1)}, f32[5,256,128]{2,1,0:T(8,128)S(1)}, f32[5,2,8,128]{3,2,1,0:T(8,128)S(1)}) custom-call(f32[5,512,128]{2,1,0:T(8,128)S(1)} %get-tuple-element.25.own, f32[5,3,8,128]{3,2,1,0:T(8,128)S(1)} %collective-permute-done.4.far, f32[5,3,8,128]{3,2,1,0:T(8,128)S(1)} %collective-permute-done.5.near, ...), custom_call_target="tpu_custom_call" | custom-call | tf_op jit(solution)/shard_map/pallas_call | solution.py:395
  24.2 1.9 %collective-permute-done.2.far = f32[5,3,8,128]{3,2,1,0:T(8,128)S(1)} collective-permute-done((f32[5,3,8,128]{3,2,1,0:T(8,128)S(1)}, f32[5,3,8,128]{3,2,1,0:T(8,128)S(1)}, u32[]{:S(2)}, u32[]{:S(2)}) %collective-permute-start.2) | collective-permute-done | bytes 61472 | tf_op jit(solution)/shard_map/ppermute | solution.py:413
  26.1 0.0 collective-permute-done.3.near
  26.1 1.7 %shard_map.63 = (f32[768,128]{1,0:T(8,128)}, f32[3,768,128]{2,1,0:T(8,128)}, f32[768,128]{1,0:T(8,128)}) custom-call(f32[5,256,128]{2,1,0:T(8,128)S(1)} %get-tuple-element.27.edges.own, f32[5,3,8,128]{3,2,1,0:T(8,128)S(1)} %collective-permute-done.2.far, f32[5,3,8,128]{3,2,1,0:T(8,128)S(1)} %collective-permute-done.3.near, ...), custom_call_target="tpu_custom_call" | custom-call | tf_op jit(solution)/shard_map/pallas_call | solution.py:395
Async XLA Ops:
  0.6 6.1 %copy-start.1 = (f32[32,24,128]{2,1,0:T(8,128)S(1)}, f32[32,24,128]{2,1,0:T(8,128)}, u32[]{:S(2)}) copy-start(f32[32,24,128]{2,1,0:T(8,128)} %density.3) | copy-start | bytes 1179652
  0.6 6.1 %copy-start = (f32[3,32,24,128]{3,2,1,0:T(8,128)S(1)}, f32[3,32,24,128]{3,2,1,0:T(8,128)}, u32[]{:S(2)}) copy-start(f32[3,32,24,128]{3,2,1,0:T(8,128)} %momentum.3) | copy-start | bytes 3538948
  0.7 6.1 %copy-start.2 = (f32[32,24,128]{2,1,0:T(8,128)S(1)}, f32[32,24,128]{2,1,0:T(8,128)}, u32[]{:S(2)}) copy-start(f32[32,24,128]{2,1,0:T(8,128)} %energy.3) | copy-start | bytes 1179652
  2.3 14.5 %collective-permute-start = (f32[5,3,32,128]{3,2,1,0:T(8,128)S(1)}, f32[5,3,32,128]{3,2,1,0:T(8,128)S(1)}, u32[]{:S(2)}, u32[]{:S(2)}) collective-permute-start(f32[5,3,32,128]{3,2,1,0:T(8,128)S(1)} %get-tuple-element.21), channel_id=1, source_target_pairs={{8,16},{24,0},{16,8},{0,24},{9,17},{25,1},{17,9},{1,25},{10,18},{2... | collective-permute-start | bytes 737288 | tf_op jit(solution)/shard_map/ppermute | solution.py:413
  6.2 11.5 %collective-permute-start.1 = (f32[5,3,32,128]{3,2,1,0:T(8,128)S(1)}, f32[5,3,32,128]{3,2,1,0:T(8,128)S(1)}, u32[]{:S(2)}, u32[]{:S(2)}) collective-permute-start(f32[5,3,32,128]{3,2,1,0:T(8,128)S(1)} %get-tuple-element.22), channel_id=1, source_target_pairs={{0,8},{16,24},{8,0},{24,16},{1,9},{17,25},{9,1},{25,17},{2,10},{18... | collective-permute-start | bytes 737288 | tf_op jit(solution)/shard_map/ppermute | solution.py:413
  12.5 9.9 %collective-permute-start.4 = (f32[5,3,8,128]{3,2,1,0:T(8,128)S(1)}, f32[5,3,8,128]{3,2,1,0:T(8,128)S(1)}, u32[]{:S(2)}, u32[]{:S(2)}) collective-permute-start(f32[5,3,8,128]{3,2,1,0:T(8,128)S(1)} %get-tuple-element.30), channel_id=1, source_target_pairs={{1,2},{3,4},{5,6},{7,0},{2,1},{4,3},{6,5},{0,7},{9,10},{11,12},{13... | collective-permute-start | bytes 184328 | tf_op jit(solution)/shard_map/ppermute | solution.py:413
  15.1 7.3 %collective-permute-start.5 = (f32[5,3,8,128]{3,2,1,0:T(8,128)S(1)}, f32[5,3,8,128]{3,2,1,0:T(8,128)S(1)}, u32[]{:S(2)}, u32[]{:S(2)}) collective-permute-start(f32[5,3,8,128]{3,2,1,0:T(8,128)S(1)} %get-tuple-element.31), channel_id=1, source_target_pairs={{0,1},{2,3},{4,5},{6,7},{1,0},{3,2},{5,4},{7,6},{8,9},{10,11},{12,... | collective-permute-start | bytes 184328 | tf_op jit(solution)/shard_map/ppermute | solution.py:413
  20.2 5.9 %collective-permute-start.2 = (f32[5,3,8,128]{3,2,1,0:T(8,128)S(1)}, f32[5,3,8,128]{3,2,1,0:T(8,128)S(1)}, u32[]{:S(2)}, u32[]{:S(2)}) collective-permute-start(f32[5,3,8,128]{3,2,1,0:T(8,128)S(1)} %get-tuple-element.28), channel_id=1, source_target_pairs={{1,2},{3,4},{5,6},{7,0},{2,1},{4,3},{6,5},{0,7},{9,10},{11,12},{13... | collective-permute-start | bytes 184328 | tf_op jit(solution)/shard_map/ppermute | solution.py:413
  22.4 3.7 %collective-permute-start.3 = (f32[5,3,8,128]{3,2,1,0:T(8,128)S(1)}, f32[5,3,8,128]{3,2,1,0:T(8,128)S(1)}, u32[]{:S(2)}, u32[]{:S(2)}) collective-permute-start(f32[5,3,8,128]{3,2,1,0:T(8,128)S(1)} %get-tuple-element.29), channel_id=1, source_target_pairs={{0,1},{2,3},{4,5},{6,7},{1,0},{3,2},{5,4},{7,6},{8,9},{10,11},{12,... | collective-permute-start | bytes 184328 | tf_op jit(solution)/shard_map/ppermute | solution.py:413

commit v3 on v2

--- a/solution.py
+++ b/solution.py
@@ -155,26 +155,20 @@
     return Received(odd, near, far), Received(odd, far, near)
 
 
-def rows_kernel(density, momentum, energy, far, near, held, arrived):
+def rows_kernel(far, density, momentum, energy, out, held, arrived):
     sources = fields_of(density, momentum, energy)
     nx, ny, nz = density.shape
-    copies = []
-    for f in range(5):
-        for side in range(2):
-            tile = sources[f].at[:, pl.ds(side * (ny - 8), 8), :]
-            copies.append(pltpu.make_async_copy(tile, held.at[side, f], arrived.at[side, f]))
+    bottom = odd_rank("gy") == far
+    start = pl.multiple_of(jnp.where(bottom, ny - 8, 0), 8)
+    copies = [pltpu.make_async_copy(s.at[:, pl.ds(start, 8), :], held.at[f], arrived.at[f]) for f, s in enumerate(sources)]
     for copy in copies:
         copy.start()
-    odd = odd_rank("gy")
     for f in range(5):
-        copies[2 * f].wait()
-        copies[2 * f + 1].wait()
-        top, bottom = (held.at[side, f].reshape(nx * 8, nz) for side in range(2))
+        copies[f].wait()
+        flat = held.at[f].reshape(nx * 8, nz)
         for r in range(halo):
-            first = top[pl.ds(r, nx, stride=8), :]
-            last = bottom[pl.ds(8 - halo + r, nx, stride=8), :]
-            far[f, r] = jnp.where(odd, last, first)
-            near[f, r] = jnp.where(odd, first, last)
+            first, last = (flat[pl.ds(at, nx, stride=8), :] for at in (r, 8 - halo + r))
+            out[f, r] = jnp.where(bottom, last, first)
 
 
 def alternate(steps, parts, others, other_parts):
@@ -301,7 +295,7 @@
     ends(turned, count, far, near)
 
 
-def edge_kernel(far, near, rim, joint, _, turned, far_end, near_end, ghost, *outers):
+def edge_kernel(near, far, rim, joint, _, turned, far_end, near_end, ghost, *outers):
     _, kept, nx, lanes = rim.shape
     kept = kept // 2
     deep = lanes // nx
@@ -351,7 +345,7 @@
         pass
 
 
-def ends_kernel(count, own, far, near, middle, joint, edges, inner, edges_middle, edges_joint, swept):
+def ends_kernel(count, own, near, far, middle, joint, edges, inner, edges_middle, edges_joint, swept):
     lanes = own.shape[-1]
     z_ends(own, far, near, middle, joint, swept, count)
 
@@ -363,7 +357,7 @@
     alternate(z_middle(edges, edges_middle, edges_joint, 2), cells, turns, 5 * count)
 
 
-def last_kernel(ny, own, far, near, middle, joint, inner, density, momentum, energy, swept, whole, sent):
+def last_kernel(ny, own, near, far, middle, joint, inner, density, momentum, energy, swept, whole, sent):
     lanes = own.shape[-1]
     nx = density.shape[0] // ny
     deep = lanes // nx
@@ -402,28 +396,24 @@
     )(*arguments)
 
 
-def exchange(axis, far, near):
+def exchange(axis, block, far):
     ranks = lax.axis_size(axis)
     if ranks % 2:
         raise ValueError("odd ring")
-    pairs = []
-    for start in (1, 0):
-        there = [(rank, (rank + 1) % ranks) for rank in range(start, ranks, 2)]
-        pairs.append(there + [(b, a) for a, b in there])
-    return lax.ppermute(far, axis, pairs[0]), lax.ppermute(near, axis, pairs[1])
-
-
-def y_rows(density, momentum, energy):
-    nx, ny, nz = density.shape
-    shape = (5, halo, nx, nz)
+    there = [(rank, (rank + 1) % ranks) for rank in range(int(far), ranks, 2)]
+    return lax.ppermute(block, axis, there + [(b, a) for a, b in there])
+
+
+def y_rows(far, fields):
+    nx, _, nz = fields[0].shape
     return pl.pallas_call(
-        rows_kernel,
-        out_shape=[pltpu.VMEM(shape, jnp.float32)] * 2,
+        functools.partial(rows_kernel, far),
+        out_shape=pltpu.VMEM((5, halo, nx, nz), jnp.float32),
         in_specs=[pl.BlockSpec(memory_space=pltpu.HBM)] * 3,
-        out_specs=[pl.BlockSpec(memory_space=pltpu.VMEM)] * 2,
-        scratch_shapes=[pltpu.VMEM((2, 5, nx, 8, nz), jnp.float32), pltpu.SemaphoreType.DMA((2, 5))],
+        out_specs=pl.BlockSpec(memory_space=pltpu.VMEM),
+        scratch_shapes=[pltpu.VMEM((5, nx, 8, nz), jnp.float32), pltpu.SemaphoreType.DMA((5,))],
         compiler_params=pltpu.CompilerParams(vmem_limit_bytes=16 * 2**20),
-    )(*(pltpu.with_memory_space_constraint(a, pltpu.HBM) for a in (density, momentum, energy)))
+    )(*(pltpu.with_memory_space_constraint(a, pltpu.HBM) for a in fields))
 
 
 def body(density, momentum, energy):
@@ -433,14 +423,15 @@
     kept = deep + halo - 1
     end = (5, halo, 8, nz)
 
-    far_rows, near_rows = exchange("gy", *y_rows(density, momentum, energy))
+    fields = (density, momentum, energy)
+    near_rows, far_rows = (exchange("gy", y_rows(far, fields), far) for far in (False, True))
     turned, far, near, rim, joint = call(
         inner_kernel,
         [(5, count * nz, nz), end, end, (5, 2 * kept, nx, nz), (5, 2, nx, nz)],
         [(5, nx * ny, nz)] + [(5, nz, nz)] * count,
-        [density, momentum, energy],
-    )
-    far, near = exchange("gz", far, near)
+        list(fields),
+    )
+    near, far = exchange("gz", near, False), exchange("gz", far, True)
     middle, faces = call(
         functools.partial(middle_kernel, count),
         [(5, count * nz, nz), (5, 2, quarters * count, nz)],
@@ -452,22 +443,22 @@
         edge_kernel,
         [(5, 2 * nz, nz), end, end],
         [(5, 2 * halo, nx, nz)] + [(5, nz, nz)] * 2,
-        [far_rows, near_rows, rim, joint, faces],
+        [near_rows, far_rows, rim, joint, faces],
         [whole] * 4 + [anywhere],
     )
-    far_edges, near_edges = exchange("gz", far_edges, near_edges)
+    near_edges, far_edges = exchange("gz", near_edges, False), exchange("gz", far_edges, True)
     inner, edges_middle, edges_faces = call(
         functools.partial(ends_kernel, count),
         [(5, count * nz, nz), (5, 2 * nz, nz), (5, 2, quarters * 2, nz)],
         [(5, count * nz, nz)],
-        [turned, far, near, middle, faces, edges],
+        [turned, near, far, middle, faces, edges],
     )
     cells = nx * ny
     outs = call(
         functools.partial(last_kernel, ny),
         [(cells, nz), (3, cells, nz), (cells, nz)],
         [(5, 2 * nz, nz), (5, cells, nz), pltpu.SemaphoreType.DMA((5,))],
-        [edges, far_edges, near_edges, edges_middle, edges_faces, inner],
+        [edges, near_edges, far_edges, edges_middle, edges_faces, inner],
         out_spec=anywhere,
     )
     return (outs[0].reshape(nx, ny, nz), outs[1].reshape(3, nx, ny, nz), outs[2].reshape(nx, ny, nz))

time: 27.9 us -> 28.9 us (1.036)
  starting transfers between devices: 9.28 us -> 10.4 us
  waiting for transfers between devices: 2.75 us -> 1.69 us
  Pallas kernels: 15 us -> 15.9 us
    ppermute x6, starting transfers between devices: 9.28 us -> 10.4 us  [exchange(): return lax.ppermute(block, axis, there + [(b, a) for a, b in there])]
    ppermute x6, waiting for transfers between devices: 2.75 us -> 1.69 us  [exchange(): return lax.ppermute(block, axis, there + [(b, a) for a, b in there])]
    pallas_call x1 -> x2, Pallas kernels: 1.61 us -> 2.48 us  [y_rows(): pl.pallas_call(functools.partial(rows_kernel, far), out_shape=pltpu.VMEM(...]
  transfers between devices with their start and end apart: 6 -> 6, of which waited for: 2 -> 1; matrix products, arithmetic and copies ran while one was open for 0% -> 0% of each run, Pallas kernels for 42% -> 45%
where the time goes in v3:
time: 28.9 us; the launch traced here: 28.8 us
  Pallas kernels  15.9 us (55%)
  starting transfers between devices  10.4 us (36%)
  waiting for transfers between devices  1.69 us (6%)
  between operations  0.73 us (3%)
    pallas_call x5, Pallas kernels, call(): pl.pallas_call(kernel, out_shape=[jax.ShapeDtypeStruct(shape, jnp.float32...  13.4 us
    ppermute x6, starting transfers between devices, exchange(): return lax.ppermute(block, axis, there + [(b, a) for a, b in there])  10.4 us
    pallas_call x2, Pallas kernels, y_rows(): pl.pallas_call(functools.partial(rows_kernel, far), out_shape=pltpu.VMEM(...  2.48 us
    ppermute x6, waiting for transfers between devices, exchange(): return lax.ppermute(block, axis, there + [(b, a) for a, b in there])  1.69 us
  transfers between devices with their start and end apart: 6, of which 1 were waited for; matrix products, arithmetic and copies ran while one was open for 0% of the time, Pallas kernels for 45%

profile of v3, /device:TPU:0, one launch (start us, length us, event | category | flops | bytes accessed | tf_op | source)
XLA Modules:
  0.0 28.8 jit_solution(9618185399268384899)
XLA Ops:
  0.6 1.2 %shard_map.58 = f32[5,3,32,128]{3,2,1,0:T(8,128)S(1)} custom-call(f32[32,24,128]{2,1,0:T(8,128)} %density.5, f32[3,32,24,128]{3,2,1,0:T(8,128)} %momentum.5, f32[32,24,128]{2,1,0:T(8,128)} %energy.5), custom_call_target="tpu_custom_call" | custom-call | tf_op jit(solution)/shard_map/pallas_call | solution.py:409
  1.9 0.0 copy-start
  1.9 0.0 copy-start.1
  1.9 0.0 copy-start.2
  1.9 3.0 %collective-permute-start = (f32[5,3,32,128]{3,2,1,0:T(8,128)S(1)}, f32[5,3,32,128]{3,2,1,0:T(8,128)S(1)}, u32[]{:S(2)}, u32[]{:S(2)}) collective-permute-start(f32[5,3,32,128]{3,2,1,0:T(8,128)S(1)} %shard_map.58), channel_id=1, source_target_pairs={{0,8},{16,24},{8,0},{24,16},{1,9},{17,25},{9,1},{25,17},{2,10},{18... | collective-permute-start | bytes 737288 | tf_op jit(solution)/shard_map/ppermute | solution.py:404
  4.9 1.2 %shard_map.59 = f32[5,3,32,128]{3,2,1,0:T(8,128)S(1)} custom-call(f32[32,24,128]{2,1,0:T(8,128)} %density.5, f32[3,32,24,128]{3,2,1,0:T(8,128)} %momentum.5, f32[32,24,128]{2,1,0:T(8,128)} %energy.5), custom_call_target="tpu_custom_call" | custom-call | tf_op jit(solution)/shard_map/pallas_call | solution.py:409
  6.2 1.6 %collective-permute-start.1 = (f32[5,3,32,128]{3,2,1,0:T(8,128)S(1)}, f32[5,3,32,128]{3,2,1,0:T(8,128)S(1)}, u32[]{:S(2)}, u32[]{:S(2)}) collective-permute-start(f32[5,3,32,128]{3,2,1,0:T(8,128)S(1)} %shard_map.59), channel_id=1, source_target_pairs={{8,16},{24,0},{16,8},{0,24},{9,17},{25,1},{17,9},{1,25},{10,18},{2... | collective-permute-start | bytes 737288 | tf_op jit(solution)/shard_map/ppermute | solution.py:404
  7.7 0.0 copy-done
  7.7 0.0 copy-done.1
  7.7 0.0 copy-done.2
  7.7 5.7 %shard_map.60 = (f32[5,512,128]{2,1,0:T(8,128)S(1)}, f32[5,3,8,128]{3,2,1,0:T(8,128)S(1)}, f32[5,3,8,128]{3,2,1,0:T(8,128)S(1)}, f32[5,12,32,128]{3,2,1,0:T(8,128)S(1)}, f32[5,2,32,128]{3,2,1,0:T(8,128)S(1)}) custom-call(f32[32,24,128]{2,1,0:T(8,128)S(1)} %copy-done.1, f32[3,32,24,128]{3,2,1,0:T(8,128)S(1)} %copy-done, f32[32,24,128]{2,1,0:T(8,128)S(1)} %copy-done.2), custom_call_target="tpu_custom_call" | custom-call | tf_op jit(solution)/shard_map/pallas_call | solution.py:389
  13.5 0.1 collective-permute-start.4
  13.5 3.7 %collective-permute-start.5 = (f32[5,3,8,128]{3,2,1,0:T(8,128)S(1)}, f32[5,3,8,128]{3,2,1,0:T(8,128)S(1)}, u32[]{:S(2)}, u32[]{:S(2)}) collective-permute-start(f32[5,3,8,128]{3,2,1,0:T(8,128)S(1)} %get-tuple-element.27), channel_id=1, source_target_pairs={{1,2},{3,4},{5,6},{7,0},{2,1},{4,3},{6,5},{0,7},{9,10},{11,12},{13... | collective-permute-start | bytes 184328 | tf_op jit(solution)/shard_map/ppermute | solution.py:404
  17.2 1.7 %shard_map.61 = (f32[5,512,128]{2,1,0:T(8,128)S(1)}, f32[5,2,16,128]{3,2,1,0:T(8,128)S(1)}) custom-call(f32[5,512,128]{2,1,0:T(8,128)S(1)} %get-tuple-element.21.own), custom_call_target="tpu_custom_call" | custom-call | tf_op jit(solution)/shard_map/pallas_call | solution.py:389
  19.0 0.0 collective-permute-done.near
  19.0 0.0 collective-permute-done.1.far
  19.0 2.5 %shard_map.62 = (f32[5,256,128]{2,1,0:T(8,128)S(1)}, f32[5,3,8,128]{3,2,1,0:T(8,128)S(1)}, f32[5,3,8,128]{3,2,1,0:T(8,128)S(1)}) custom-call(f32[5,3,32,128]{3,2,1,0:T(8,128)S(1)} %collective-permute-done.near, f32[5,3,32,128]{3,2,1,0:T(8,128)S(1)} %collective-permute-done.1.far, f32[5,12,32,128]{3,2,1,0:T(8,128)S(1)} %get-tuple-element.19.rim, ...), custom_call_target="tpu_custom_call" | custom-call | tf_op jit(solution)/shard_map/pallas_call | solution.py:389
  21.5 0.1 collective-permute-start.2
  21.6 2.0 %collective-permute-start.3 = (f32[5,3,8,128]{3,2,1,0:T(8,128)S(1)}, f32[5,3,8,128]{3,2,1,0:T(8,128)S(1)}, u32[]{:S(2)}, u32[]{:S(2)}) collective-permute-start(f32[5,3,8,128]{3,2,1,0:T(8,128)S(1)} %get-tuple-element.25), channel_id=1, source_target_pairs={{1,2},{3,4},{5,6},{7,0},{2,1},{4,3},{6,5},{0,7},{9,10},{11,12},{13... | collective-permute-start | bytes 184328 | tf_op jit(solution)/shard_map/ppermute | solution.py:404
  23.6 0.0 collective-permute-done.4.near
  23.6 0.0 collective-permute-done.5.far
  23.6 1.8 %shard_map.63 = (f32[5,512,128]{2,1,0:T(8,128)S(1)}, f32[5,256,128]{2,1,0:T(8,128)S(1)}, f32[5,2,8,128]{3,2,1,0:T(8,128)S(1)}) custom-call(f32[5,512,128]{2,1,0:T(8,128)S(1)} %get-tuple-element.21.own, f32[5,3,8,128]{3,2,1,0:T(8,128)S(1)} %collective-permute-done.4.near, f32[5,3,8,128]{3,2,1,0:T(8,128)S(1)} %collective-permute-done.5.far, ...), custom_call_target="tpu_custom_call" | custom-call | tf_op jit(solution)/shard_map/pallas_call | solution.py:389
  25.4 0.0 collective-permute-done.2.near
  25.4 1.7 %collective-permute-done.3.far = f32[5,3,8,128]{3,2,1,0:T(8,128)S(1)} collective-permute-done((f32[5,3,8,128]{3,2,1,0:T(8,128)S(1)}, f32[5,3,8,128]{3,2,1,0:T(8,128)S(1)}, u32[]{:S(2)}, u32[]{:S(2)}) %collective-permute-start.3) | collective-permute-done | bytes 61472 | tf_op jit(solution)/shard_map/ppermute | solution.py:404
  27.1 1.7 %shard_map.64 = (f32[768,128]{1,0:T(8,128)}, f32[3,768,128]{2,1,0:T(8,128)}, f32[768,128]{1,0:T(8,128)}) custom-call(f32[5,256,128]{2,1,0:T(8,128)S(1)} %get-tuple-element.23.edges.own, f32[5,3,8,128]{3,2,1,0:T(8,128)S(1)} %collective-permute-done.2.near, f32[5,3,8,128]{3,2,1,0:T(8,128)S(1)} %collective-permute-done.3.far, ...), custom_call_target="tpu_custom_call" | custom-call | tf_op jit(solution)/shard_map/pallas_call | solution.py:389
Async XLA Ops:
  1.9 5.8 %copy-start = (f32[3,32,24,128]{3,2,1,0:T(8,128)S(1)}, f32[3,32,24,128]{3,2,1,0:T(8,128)}, u32[]{:S(2)}) copy-start(f32[3,32,24,128]{3,2,1,0:T(8,128)} %momentum.5) | copy-start | bytes 3538948
  1.9 5.8 %copy-start.1 = (f32[32,24,128]{2,1,0:T(8,128)S(1)}, f32[32,24,128]{2,1,0:T(8,128)}, u32[]{:S(2)}) copy-start(f32[32,24,128]{2,1,0:T(8,128)} %density.5) | copy-start | bytes 1179652
  1.9 5.8 %copy-start.2 = (f32[32,24,128]{2,1,0:T(8,128)S(1)}, f32[32,24,128]{2,1,0:T(8,128)}, u32[]{:S(2)}) copy-start(f32[32,24,128]{2,1,0:T(8,128)} %energy.5) | copy-start | bytes 1179652
  1.9 17.1 %collective-permute-start = (f32[5,3,32,128]{3,2,1,0:T(8,128)S(1)}, f32[5,3,32,128]{3,2,1,0:T(8,128)S(1)}, u32[]{:S(2)}, u32[]{:S(2)}) collective-permute-start(f32[5,3,32,128]{3,2,1,0:T(8,128)S(1)} %shard_map.58), channel_id=1, source_target_pairs={{0,8},{16,24},{8,0},{24,16},{1,9},{17,25},{9,1},{25,17},{2,10},{18... | collective-permute-start | bytes 737288 | tf_op jit(solution)/shard_map/ppermute | solution.py:404
  6.2 12.8 %collective-permute-start.1 = (f32[5,3,32,128]{3,2,1,0:T(8,128)S(1)}, f32[5,3,32,128]{3,2,1,0:T(8,128)S(1)}, u32[]{:S(2)}, u32[]{:S(2)}) collective-permute-start(f32[5,3,32,128]{3,2,1,0:T(8,128)S(1)} %shard_map.59), channel_id=1, source_target_pairs={{8,16},{24,0},{16,8},{0,24},{9,17},{25,1},{17,9},{1,25},{10,18},{2... | collective-permute-start | bytes 737288 | tf_op jit(solution)/shard_map/ppermute | solution.py:404
  13.5 10.1 %collective-permute-start.4 = (f32[5,3,8,128]{3,2,1,0:T(8,128)S(1)}, f32[5,3,8,128]{3,2,1,0:T(8,128)S(1)}, u32[]{:S(2)}, u32[]{:S(2)}) collective-permute-start(f32[5,3,8,128]{3,2,1,0:T(8,128)S(1)} %get-tuple-element.26), channel_id=1, source_target_pairs={{0,1},{2,3},{4,5},{6,7},{1,0},{3,2},{5,4},{7,6},{8,9},{10,11},{12,... | collective-permute-start | bytes 184328 | tf_op jit(solution)/shard_map/ppermute | solution.py:404
  13.5 10.0 %collective-permute-start.5 = (f32[5,3,8,128]{3,2,1,0:T(8,128)S(1)}, f32[5,3,8,128]{3,2,1,0:T(8,128)S(1)}, u32[]{:S(2)}, u32[]{:S(2)}) collective-permute-start(f32[5,3,8,128]{3,2,1,0:T(8,128)S(1)} %get-tuple-element.27), channel_id=1, source_target_pairs={{1,2},{3,4},{5,6},{7,0},{2,1},{4,3},{6,5},{0,7},{9,10},{11,12},{13... | collective-permute-start | bytes 184328 | tf_op jit(solution)/shard_map/ppermute | solution.py:404
  21.5 3.9 %collective-permute-start.2 = (f32[5,3,8,128]{3,2,1,0:T(8,128)S(1)}, f32[5,3,8,128]{3,2,1,0:T(8,128)S(1)}, u32[]{:S(2)}, u32[]{:S(2)}) collective-permute-start(f32[5,3,8,128]{3,2,1,0:T(8,128)S(1)} %get-tuple-element.24), channel_id=1, source_target_pairs={{0,1},{2,3},{4,5},{6,7},{1,0},{3,2},{5,4},{7,6},{8,9},{10,11},{12,... | collective-permute-start | bytes 184328 | tf_op jit(solution)/shard_map/ppermute | solution.py:404
  21.6 5.5 %collective-permute-start.3 = (f32[5,3,8,128]{3,2,1,0:T(8,128)S(1)}, f32[5,3,8,128]{3,2,1,0:T(8,128)S(1)}, u32[]{:S(2)}, u32[]{:S(2)}) collective-permute-start(f32[5,3,8,128]{3,2,1,0:T(8,128)S(1)} %get-tuple-element.25), channel_id=1, source_target_pairs={{1,2},{3,4},{5,6},{7,0},{2,1},{4,3},{6,5},{0,7},{9,10},{11,12},{13... | collective-permute-start | bytes 184328 | tf_op jit(solution)/shard_map/ppermute | solution.py:404

commit v4 on v2

--- a/solution.py
+++ b/solution.py
@@ -262,7 +262,7 @@
                 swept[f, at, :] = value
 
 
-def inner_kernel(density, momentum, energy, turned, far, near, rim, joint, held, *strips):
+def inner_kernel(density, momentum, energy, turned, far, near, rim, beside, joint, held, *strips):
     nx, ny, lanes = density.shape
     deep = lanes // nx
     sources = fields_of(density, momentum, energy)
@@ -278,13 +278,16 @@
     def sweep(tile):
         some = row(tile * 8)
         line = Line(lambda i: [held[f, pl.ds(tile * (8 * ny) + i, 8, stride=ny), :] for f in range(5)], 1)
-        for i in range(deep, ny - deep):
+        for i in range(halo, ny - halo):
             for f, value in enumerate(line.swept(i)):
-                strips[tile][f, row((i - deep) * 8), :] = value
+                if deep <= i < ny - deep:
+                    strips[tile][f, row((i - deep) * 8), :] = value
+                else:
+                    beside[f, i - halo if i < deep else i - ny + 2 * deep - halo, some, :] = value
             yield
         for f in range(5):
-            joint[f, 0, some, :] = line.flux(deep - 1)[f]
-            joint[f, 1, some, :] = line.flux(ny - deep - 1)[f]
+            joint[f, 0, some, :] = line.flux(halo - 1)[f]
+            joint[f, 1, some, :] = line.flux(ny - halo - 1)[f]
         kept = deep + halo - 1
         for r in range(kept):
             for f, (a, b) in enumerate(zip(line.load(r), line.load(ny - kept + r))):
@@ -294,14 +297,14 @@
     count = len(strips)
     turns = iter(())
     for tile in range(count):
-        alternate(sweep(tile), ny - 2 * deep, turns, 5)
+        alternate(sweep(tile), ny - 2 * halo, turns, 5)
         turns = turn_in(strips[tile], turned, count, tile)
     for _ in turns:
         pass
     ends(turned, count, far, near)
 
 
-def edge_kernel(far, near, rim, joint, _, turned, far_end, near_end, ghost, *outers):
+def edge_kernel(far, near, rim, beside, joint, _, turned, far_end, near_end, ghost, *outers):
     _, kept, nx, lanes = rim.shape
     kept = kept // 2
     deep = lanes // nx
@@ -330,10 +333,16 @@
                     return [source[f, at, some, :] for f in range(5)]
 
                 line = Line(load, 1)
-                known = deep - 1 if side == 0 else -1
+                known = halo - 1 if side == 0 else deep - halo - 1
                 line.known[("f", known)] = [joint[f, side, some, :] for f in range(5)]
                 for i in range(deep):
-                    for f, value in enumerate(line.swept(i)):
+                    if side == 0 and i >= halo:
+                        values = [beside[f, i - halo, some, :] for f in range(5)]
+                    elif side == 1 and i < deep - halo:
+                        values = [beside[f, i + deep - halo, some, :] for f in range(5)]
+                    else:
+                        values = line.swept(i)
+                    for f, value in enumerate(values):
                         outers[block][f, row(((half * 2 + side) * deep + i) * 8), :] = value
                     yield
 
@@ -434,9 +443,9 @@
     end = (5, halo, 8, nz)
 
     far_rows, near_rows = exchange("gy", *y_rows(density, momentum, energy))
-    turned, far, near, rim, joint = call(
+    turned, far, near, rim, beside, joint = call(
         inner_kernel,
-        [(5, count * nz, nz), end, end, (5, 2 * kept, nx, nz), (5, 2, nx, nz)],
+        [(5, count * nz, nz), end, end, (5, 2 * kept, nx, nz), (5, 2 * (deep - halo), nx, nz), (5, 2, nx, nz)],
         [(5, nx * ny, nz)] + [(5, nz, nz)] * count,
         [density, momentum, energy],
     )
@@ -452,8 +461,8 @@
         edge_kernel,
         [(5, 2 * nz, nz), end, end],
         [(5, 2 * halo, nx, nz)] + [(5, nz, nz)] * 2,
-        [far_rows, near_rows, rim, joint, faces],
-        [whole] * 4 + [anywhere],
+        [far_rows, near_rows, rim, beside, joint, faces],
+        [whole] * 5 + [anywhere],
     )
     far_edges, near_edges = exchange("gz", far_edges, near_edges)
     inner, edges_middle, edges_faces = call(

time: 27.9 us -> 27.7 us (level)
  transfers between devices with their start and end apart: 6 -> 6, of which waited for: 2 -> 2; matrix products, arithmetic and copies ran while one was open for 0% -> 0% of each run, Pallas kernels for 42% -> 43%
where the time goes in v4:
time: 27.7 us; the launch traced here: 27.5 us
  Pallas kernels  15 us (54%)
  starting transfers between devices  9.28 us (34%)
  waiting for transfers between devices  2.48 us (9%)
  between operations  0.7 us (3%)
    pallas_call x5, Pallas kernels, call(): pl.pallas_call(kernel, out_shape=[jax.ShapeDtypeStruct(shape, jnp.float32...  13.4 us
    ppermute x3, starting transfers between devices, exchange(): lax.ppermute(far, axis, pairs[0])  8.74 us
    ppermute x3, waiting for transfers between devices, exchange(): lax.ppermute(far, axis, pairs[0])  1.86 us
    pallas_call x1, Pallas kernels, y_rows(): pl.pallas_call(rows_kernel, out_shape=[pltpu.VMEM(shape, jnp.float32)] *...  1.61 us
    ppermute x3, waiting for transfers between devices, exchange(): lax.ppermute(near, axis, pairs[1])  0.63 us
  transfers between devices with their start and end apart: 6, of which 2 were waited for; matrix products, arithmetic and copies ran while one was open for 0% of the time, Pallas kernels for 43%

profile of v4, /device:TPU:0, one launch (start us, length us, event | category | flops | bytes accessed | tf_op | source)
XLA Modules:
  0.0 27.5 jit_solution(13101528694002549604)
XLA Ops:
  0.6 0.0 copy-start.1
  0.6 0.0 copy-start
  0.7 0.0 copy-start.2
  0.7 1.6 %shard_map.58 = (f32[5,3,32,128]{3,2,1,0:T(8,128)S(1)}, f32[5,3,32,128]{3,2,1,0:T(8,128)S(1)}) custom-call(f32[32,24,128]{2,1,0:T(8,128)} %density.3, f32[3,32,24,128]{3,2,1,0:T(8,128)} %momentum.3, f32[32,24,128]{2,1,0:T(8,128)} %energy.3), custom_call_target="tpu_custom_call" | custom-call | tf_op jit(solution)/shard_map/pallas_call | solution.py:428
  2.3 4.0 %collective-permute-start = (f32[5,3,32,128]{3,2,1,0:T(8,128)S(1)}, f32[5,3,32,128]{3,2,1,0:T(8,128)S(1)}, u32[]{:S(2)}, u32[]{:S(2)}) collective-permute-start(f32[5,3,32,128]{3,2,1,0:T(8,128)S(1)} %get-tuple-element.22), channel_id=1, source_target_pairs={{8,16},{24,0},{16,8},{0,24},{9,17},{25,1},{17,9},{1,25},{10,18},{2... | collective-permute-start | bytes 737288 | tf_op jit(solution)/shard_map/ppermute | solution.py:422
  6.2 0.5 %collective-permute-start.1 = (f32[5,3,32,128]{3,2,1,0:T(8,128)S(1)}, f32[5,3,32,128]{3,2,1,0:T(8,128)S(1)}, u32[]{:S(2)}, u32[]{:S(2)}) collective-permute-start(f32[5,3,32,128]{3,2,1,0:T(8,128)S(1)} %get-tuple-element.23), channel_id=1, source_target_pairs={{0,8},{16,24},{8,0},{24,16},{1,9},{17,25},{9,1},{25,17},{2,10},{18... | collective-permute-start | bytes 737288 | tf_op jit(solution)/shard_map/ppermute | solution.py:422
  6.8 0.0 copy-done.1
  6.8 0.0 copy-done
  6.8 0.0 copy-done.2
  6.8 6.0 %shard_map.59 = (f32[5,512,128]{2,1,0:T(8,128)S(1)}, f32[5,3,8,128]{3,2,1,0:T(8,128)S(1)}, f32[5,3,8,128]{3,2,1,0:T(8,128)S(1)}, f32[5,12,32,128]{3,2,1,0:T(8,12...) custom-call(f32[32,24,128]{2,1,0:T(8,128)S(1)} %copy-done.1, f32[3,32,24,128]{3,2,1,0:T(8,128)S(1)} %copy-done, ...), custom_call_target="tpu_custom_call" | custom-call | tf_op jit(solution)/shard_map/pallas_call | solution.py:404
  12.8 2.5 %collective-permute-start.4 = (f32[5,3,8,128]{3,2,1,0:T(8,128)S(1)}, f32[5,3,8,128]{3,2,1,0:T(8,128)S(1)}, u32[]{:S(2)}, u32[]{:S(2)}) collective-permute-start(f32[5,3,8,128]{3,2,1,0:T(8,128)S(1)} %get-tuple-element.32), channel_id=1, source_target_pairs={{1,2},{3,4},{5,6},{7,0},{2,1},{4,3},{6,5},{0,7},{9,10},{11,12},{13... | collective-permute-start | bytes 184328 | tf_op jit(solution)/shard_map/ppermute | solution.py:422
  15.3 0.0 collective-permute-start.5
  15.3 1.7 %shard_map.60 = (f32[5,512,128]{2,1,0:T(8,128)S(1)}, f32[5,2,16,128]{3,2,1,0:T(8,128)S(1)}) custom-call(f32[5,512,128]{2,1,0:T(8,128)S(1)} %get-tuple-element.27.own), custom_call_target="tpu_custom_call" | custom-call | tf_op jit(solution)/shard_map/pallas_call | solution.py:404
  17.1 0.0 collective-permute-done.far
  17.1 0.6 %collective-permute-done.1.near = f32[5,3,32,128]{3,2,1,0:T(8,128)S(1)} collective-permute-done((f32[5,3,32,128]{3,2,1,0:T(8,128)S(1)}, f32[5,3,32,128]{3,2,1,0:T(8,128)S(1)}, u32[]{:S(2)}, u32[]{:S(2)}) %collective-permute-start.1) | collective-permute-done | bytes 245792 | tf_op jit(solution)/shard_map/ppermute | solution.py:422
  17.7 2.2 %shard_map.61 = (f32[5,256,128]{2,1,0:T(8,128)S(1)}, f32[5,3,8,128]{3,2,1,0:T(8,128)S(1)}, f32[5,3,8,128]{3,2,1,0:T(8,128)S(1)}) custom-call(f32[5,3,32,128]{3,2,1,0:T(8,128)S(1)} %collective-permute-done.far, f32[5,3,32,128]{3,2,1,0:T(8,128)S(1)} %collective-permute-done.1.near, f32[5,12,32,128]{3,2,1,0:T(8,128)S(1)} %get-tuple-element.24.rim, ...), custom_call_target="tpu_custom_call" | custom-call | tf_op jit(solution)/shard_map/pallas_call | solution.py:404
  19.9 2.2 %collective-permute-start.2 = (f32[5,3,8,128]{3,2,1,0:T(8,128)S(1)}, f32[5,3,8,128]{3,2,1,0:T(8,128)S(1)}, u32[]{:S(2)}, u32[]{:S(2)}) collective-permute-start(f32[5,3,8,128]{3,2,1,0:T(8,128)S(1)} %get-tuple-element.30), channel_id=1, source_target_pairs={{1,2},{3,4},{5,6},{7,0},{2,1},{4,3},{6,5},{0,7},{9,10},{11,12},{13... | collective-permute-start | bytes 184328 | tf_op jit(solution)/shard_map/ppermute | solution.py:422
  22.1 0.0 collective-permute-start.3
  22.1 0.0 collective-permute-done.4.far
  22.1 0.0 collective-permute-done.5.near
  22.2 1.8 %shard_map.62 = (f32[5,512,128]{2,1,0:T(8,128)S(1)}, f32[5,256,128]{2,1,0:T(8,128)S(1)}, f32[5,2,8,128]{3,2,1,0:T(8,128)S(1)}) custom-call(f32[5,512,128]{2,1,0:T(8,128)S(1)} %get-tuple-element.27.own, f32[5,3,8,128]{3,2,1,0:T(8,128)S(1)} %collective-permute-done.4.far, f32[5,3,8,128]{3,2,1,0:T(8,128)S(1)} %collective-permute-done.5.near, ...), custom_call_target="tpu_custom_call" | custom-call | tf_op jit(solution)/shard_map/pallas_call | solution.py:404
  24.0 1.9 %collective-permute-done.2.far = f32[5,3,8,128]{3,2,1,0:T(8,128)S(1)} collective-permute-done((f32[5,3,8,128]{3,2,1,0:T(8,128)S(1)}, f32[5,3,8,128]{3,2,1,0:T(8,128)S(1)}, u32[]{:S(2)}, u32[]{:S(2)}) %collective-permute-start.2) | collective-permute-done | bytes 61472 | tf_op jit(solution)/shard_map/ppermute | solution.py:422
  25.8 0.0 collective-permute-done.3.near
  25.8 1.7 %shard_map.63 = (f32[768,128]{1,0:T(8,128)}, f32[3,768,128]{2,1,0:T(8,128)}, f32[768,128]{1,0:T(8,128)}) custom-call(f32[5,256,128]{2,1,0:T(8,128)S(1)} %get-tuple-element.29.edges.own, f32[5,3,8,128]{3,2,1,0:T(8,128)S(1)} %collective-permute-done.2.far, f32[5,3,8,128]{3,2,1,0:T(8,128)S(1)} %collective-permute-done.3.near, ...), custom_call_target="tpu_custom_call" | custom-call | tf_op jit(solution)/shard_map/pallas_call | solution.py:404
Async XLA Ops:
  0.6 6.1 %copy-start.1 = (f32[32,24,128]{2,1,0:T(8,128)S(1)}, f32[32,24,128]{2,1,0:T(8,128)}, u32[]{:S(2)}) copy-start(f32[32,24,128]{2,1,0:T(8,128)} %density.3) | copy-start | bytes 1179652
  0.6 6.1 %copy-start = (f32[3,32,24,128]{3,2,1,0:T(8,128)S(1)}, f32[3,32,24,128]{3,2,1,0:T(8,128)}, u32[]{:S(2)}) copy-start(f32[3,32,24,128]{3,2,1,0:T(8,128)} %momentum.3) | copy-start | bytes 3538948
  0.7 6.1 %copy-start.2 = (f32[32,24,128]{2,1,0:T(8,128)S(1)}, f32[32,24,128]{2,1,0:T(8,128)}, u32[]{:S(2)}) copy-start(f32[32,24,128]{2,1,0:T(8,128)} %energy.3) | copy-start | bytes 1179652
  2.3 14.8 %collective-permute-start = (f32[5,3,32,128]{3,2,1,0:T(8,128)S(1)}, f32[5,3,32,128]{3,2,1,0:T(8,128)S(1)}, u32[]{:S(2)}, u32[]{:S(2)}) collective-permute-start(f32[5,3,32,128]{3,2,1,0:T(8,128)S(1)} %get-tuple-element.22), channel_id=1, source_target_pairs={{8,16},{24,0},{16,8},{0,24},{9,17},{25,1},{17,9},{1,25},{10,18},{2... | collective-permute-start | bytes 737288 | tf_op jit(solution)/shard_map/ppermute | solution.py:422
  6.2 11.5 %collective-permute-start.1 = (f32[5,3,32,128]{3,2,1,0:T(8,128)S(1)}, f32[5,3,32,128]{3,2,1,0:T(8,128)S(1)}, u32[]{:S(2)}, u32[]{:S(2)}) collective-permute-start(f32[5,3,32,128]{3,2,1,0:T(8,128)S(1)} %get-tuple-element.23), channel_id=1, source_target_pairs={{0,8},{16,24},{8,0},{24,16},{1,9},{17,25},{9,1},{25,17},{2,10},{18... | collective-permute-start | bytes 737288 | tf_op jit(solution)/shard_map/ppermute | solution.py:422
  12.8 9.4 %collective-permute-start.4 = (f32[5,3,8,128]{3,2,1,0:T(8,128)S(1)}, f32[5,3,8,128]{3,2,1,0:T(8,128)S(1)}, u32[]{:S(2)}, u32[]{:S(2)}) collective-permute-start(f32[5,3,8,128]{3,2,1,0:T(8,128)S(1)} %get-tuple-element.32), channel_id=1, source_target_pairs={{1,2},{3,4},{5,6},{7,0},{2,1},{4,3},{6,5},{0,7},{9,10},{11,12},{13... | collective-permute-start | bytes 184328 | tf_op jit(solution)/shard_map/ppermute | solution.py:422
  15.3 6.8 %collective-permute-start.5 = (f32[5,3,8,128]{3,2,1,0:T(8,128)S(1)}, f32[5,3,8,128]{3,2,1,0:T(8,128)S(1)}, u32[]{:S(2)}, u32[]{:S(2)}) collective-permute-start(f32[5,3,8,128]{3,2,1,0:T(8,128)S(1)} %get-tuple-element.33), channel_id=1, source_target_pairs={{0,1},{2,3},{4,5},{6,7},{1,0},{3,2},{5,4},{7,6},{8,9},{10,11},{12,... | collective-permute-start | bytes 184328 | tf_op jit(solution)/shard_map/ppermute | solution.py:422
  19.9 5.9 %collective-permute-start.2 = (f32[5,3,8,128]{3,2,1,0:T(8,128)S(1)}, f32[5,3,8,128]{3,2,1,0:T(8,128)S(1)}, u32[]{:S(2)}, u32[]{:S(2)}) collective-permute-start(f32[5,3,8,128]{3,2,1,0:T(8,128)S(1)} %get-tuple-element.30), channel_id=1, source_target_pairs={{1,2},{3,4},{5,6},{7,0},{2,1},{4,3},{6,5},{0,7},{9,10},{11,12},{13... | collective-permute-start | bytes 184328 | tf_op jit(solution)/shard_map/ppermute | solution.py:422
  22.1 3.7 %collective-permute-start.3 = (f32[5,3,8,128]{3,2,1,0:T(8,128)S(1)}, f32[5,3,8,128]{3,2,1,0:T(8,128)S(1)}, u32[]{:S(2)}, u32[]{:S(2)}) collective-permute-start(f32[5,3,8,128]{3,2,1,0:T(8,128)S(1)} %get-tuple-element.31), channel_id=1, source_target_pairs={{0,1},{2,3},{4,5},{6,7},{1,0},{3,2},{5,4},{7,6},{8,9},{10,11},{12,... | collective-permute-start | bytes 184328 | tf_op jit(solution)/shard_map/ppermute | solution.py:422

commit v5 on v4

--- a/solution.py
+++ b/solution.py
@@ -207,14 +207,24 @@
 
 
 def ends(turned, count, far, near):
-    span = turned.shape[1] // (quarters * count)
+    width = quarters * count
+    span = turned.shape[1] // width
     odd = odd_rank("gz")
     for f in range(5):
         for k in range(halo):
-            upward = turned[f, row((span - halo + k + 1) * quarters * count - 8), :]
-            downward = turned[f, row(k * quarters * count), :]
-            far[f, k] = jnp.where(odd, upward, downward)
-            near[f, k] = jnp.where(odd, downward, upward)
+            upward = turned[f, pl.ds((span - halo + k + 1) * width - count, count), :]
+            downward = turned[f, pl.ds(k * width, count), :]
+            at = pl.ds((f * halo + k) * count, count)
+            far[at, :] = jnp.where(odd, upward, downward)
+            near[at, :] = jnp.where(odd, downward, upward)
+
+
+def placed(ends, f, k, count, at):
+    first = (f * halo + k) * count
+    start = min(max(first - at, 0), 5 * halo * count - 8)
+    window = ends[row(start), :]
+    shift = (at + start - first) % 8
+    return pltpu.roll(window, shift, 0) if shift else window
 
 
 def z_lines(own, count, left=None, right=None):
@@ -229,11 +239,11 @@
             if i < 0:
                 fields = [own[f, row((i + span) * width + start - count), :] for f in range(5)]
                 if start == 0:
-                    fields = [jnp.where(place < count, pltpu.roll(left[f, i + halo], count, 0), a) for f, a in enumerate(fields)]
+                    fields = [jnp.where(place < count, placed(left, f, i + halo, count, 0), a) for f, a in enumerate(fields)]
                 return fields
             fields = [own[f, row((i - span) * width + start + count), :] for f in range(5)]
             if start + 8 == width:
-                fields = [jnp.where(place >= 8 - count, pltpu.roll(right[f, i - span], 8 - count, 0), a) for f, a in enumerate(fields)]
+                fields = [jnp.where(place >= 8 - count, placed(right, f, i - span, count, 8 - count), a) for f, a in enumerate(fields)]
             return fields
 
         yield start, span, Line(load, 2)
@@ -440,12 +450,11 @@
     deep = nz // nx
     count = ny // deep - 2
     kept = deep + halo - 1
-    end = (5, halo, 8, nz)
 
     far_rows, near_rows = exchange("gy", *y_rows(density, momentum, energy))
     turned, far, near, rim, beside, joint = call(
         inner_kernel,
-        [(5, count * nz, nz), end, end, (5, 2 * kept, nx, nz), (5, 2 * (deep - halo), nx, nz), (5, 2, nx, nz)],
+        [(5, count * nz, nz)] + [(5 * halo * count, nz)] * 2 + [(5, 2 * kept, nx, nz), (5, 2 * (deep - halo), nx, nz), (5, 2, nx, nz)],
         [(5, nx * ny, nz)] + [(5, nz, nz)] * count,
         [density, momentum, energy],
     )
@@ -459,7 +468,7 @@
     whole, anywhere = (pl.BlockSpec(memory_space=space) for space in (pltpu.VMEM, pl.ANY))
     edges, far_edges, near_edges = call(
         edge_kernel,
-        [(5, 2 * nz, nz), end, end],
+        [(5, 2 * nz, nz)] + [(5 * halo * 2, nz)] * 2,
         [(5, 2 * halo, nx, nz)] + [(5, nz, nz)] * 2,
         [far_rows, near_rows, rim, beside, joint, faces],
         [whole] * 5 + [anywhere],

time: 27.7 us -> 26.8 us (0.968)
  waiting for transfers between devices: 2.48 us -> 1.56 us
    ppermute x3, waiting for transfers between devices: 1.86 us -> 0.96 us  [exchange(): lax.ppermute(far, axis, pairs[0])]
  transfers between devices with their start and end apart: 6 -> 6, of which waited for: 2 -> 2; matrix products, arithmetic and copies ran while one was open for 0% -> 0% of each run, Pallas kernels for 43% -> 44%
where the time goes in v5:
time: 26.8 us; the launch traced here: 26.6 us
  Pallas kernels  15.1 us (56%)
  starting transfers between devices  9.28 us (35%)
  waiting for transfers between devices  1.56 us (6%)
  between operations  0.7 us (3%)
    pallas_call x5, Pallas kernels, call(): pl.pallas_call(kernel, out_shape=[jax.ShapeDtypeStruct(shape, jnp.float32...  13.5 us
    ppermute x3, starting transfers between devices, exchange(): lax.ppermute(far, axis, pairs[0])  8.74 us
    pallas_call x1, Pallas kernels, y_rows(): pl.pallas_call(rows_kernel, out_shape=[pltpu.VMEM(shape, jnp.float32)] *...  1.61 us
    ppermute x3, waiting for transfers between devices, exchange(): lax.ppermute(far, axis, pairs[0])  0.96 us
    ppermute x3, waiting for transfers between devices, exchange(): lax.ppermute(near, axis, pairs[1])  0.6 us
    ppermute x3, starting transfers between devices, exchange(): lax.ppermute(near, axis, pairs[1])  0.54 us
  transfers between devices with their start and end apart: 6, of which 2 were waited for; matrix products, arithmetic and copies ran while one was open for 0% of the time, Pallas kernels for 44%

profile of v5, /device:TPU:0, one launch (start us, length us, event | category | flops | bytes accessed | tf_op | source)
XLA Modules:
  0.0 26.6 jit_solution(5214493162577017122)
XLA Ops:
  0.6 0.0 copy-start.1
  0.6 0.0 copy-start
  0.7 0.0 copy-start.2
  0.7 1.6 %shard_map.58 = (f32[5,3,32,128]{3,2,1,0:T(8,128)S(1)}, f32[5,3,32,128]{3,2,1,0:T(8,128)S(1)}) custom-call(f32[32,24,128]{2,1,0:T(8,128)} %density.3, f32[3,32,24,128]{3,2,1,0:T(8,128)} %momentum.3, f32[32,24,128]{2,1,0:T(8,128)} %energy.3), custom_call_target="tpu_custom_call" | custom-call | tf_op jit(solution)/shard_map/pallas_call | solution.py:438
  2.3 4.0 %collective-permute-start = (f32[5,3,32,128]{3,2,1,0:T(8,128)S(1)}, f32[5,3,32,128]{3,2,1,0:T(8,128)S(1)}, u32[]{:S(2)}, u32[]{:S(2)}) collective-permute-start(f32[5,3,32,128]{3,2,1,0:T(8,128)S(1)} %get-tuple-element.22), channel_id=1, source_target_pairs={{8,16},{24,0},{16,8},{0,24},{9,17},{25,1},{17,9},{1,25},{10,18},{2... | collective-permute-start | bytes 737288 | tf_op jit(solution)/shard_map/ppermute | solution.py:432
  6.2 0.5 %collective-permute-start.1 = (f32[5,3,32,128]{3,2,1,0:T(8,128)S(1)}, f32[5,3,32,128]{3,2,1,0:T(8,128)S(1)}, u32[]{:S(2)}, u32[]{:S(2)}) collective-permute-start(f32[5,3,32,128]{3,2,1,0:T(8,128)S(1)} %get-tuple-element.23), channel_id=1, source_target_pairs={{0,8},{16,24},{8,0},{24,16},{1,9},{17,25},{9,1},{25,17},{2,10},{18... | collective-permute-start | bytes 737288 | tf_op jit(solution)/shard_map/ppermute | solution.py:432
  6.8 0.0 copy-done.1
  6.8 0.0 copy-done
  6.8 0.0 copy-done.2
  6.8 6.0 %shard_map.59 = (f32[5,512,128]{2,1,0:T(8,128)S(1)}, f32[60,128]{1,0:T(8,128)S(1)}, f32[60,128]{1,0:T(8,128)S(1)}, f32[5,12,32,128]{3,2,1,0:T(8,128)S(1)}, f32[5...) custom-call(f32[32,24,128]{2,1,0:T(8,128)S(1)} %copy-done.1, f32[3,32,24,128]{3,2,1,0:T(8,128)S(1)} %copy-done, ...), custom_call_target="tpu_custom_call" | custom-call | tf_op jit(solution)/shard_map/pallas_call | solution.py:414
  12.8 2.5 %collective-permute-start.4 = (f32[60,128]{1,0:T(8,128)S(1)}, f32[60,128]{1,0:T(8,128)S(1)}, u32[]{:S(2)}, u32[]{:S(2)}) collective-permute-start(f32[60,128]{1,0:T(8,128)S(1)} %get-tuple-element.32), channel_id=1, source_target_pairs={{1,2},{3,4},{5,6},{7,0},{2,1},{4,3},{6,5},{0,7},{9,10},{11,12},{13... | collective-permute-start | bytes 92168 | tf_op jit(solution)/shard_map/ppermute | solution.py:432
  15.3 0.0 collective-permute-start.5
  15.3 1.8 %shard_map.60 = (f32[5,512,128]{2,1,0:T(8,128)S(1)}, f32[5,2,16,128]{3,2,1,0:T(8,128)S(1)}) custom-call(f32[5,512,128]{2,1,0:T(8,128)S(1)} %get-tuple-element.27.own), custom_call_target="tpu_custom_call" | custom-call | tf_op jit(solution)/shard_map/pallas_call | solution.py:414
  17.1 0.0 collective-permute-done.far
  17.1 0.6 %collective-permute-done.1.near = f32[5,3,32,128]{3,2,1,0:T(8,128)S(1)} collective-permute-done((f32[5,3,32,128]{3,2,1,0:T(8,128)S(1)}, f32[5,3,32,128]{3,2,1,0:T(8,128)S(1)}, u32[]{:S(2)}, u32[]{:S(2)}) %collective-permute-start.1) | collective-permute-done | bytes 245792 | tf_op jit(solution)/shard_map/ppermute | solution.py:432
  17.7 2.2 %shard_map.61 = (f32[5,256,128]{2,1,0:T(8,128)S(1)}, f32[30,128]{1,0:T(8,128)S(1)}, f32[30,128]{1,0:T(8,128)S(1)}) custom-call(f32[5,3,32,128]{3,2,1,0:T(8,128)S(1)} %collective-permute-done.far, f32[5,3,32,128]{3,2,1,0:T(8,128)S(1)} %collective-permute-done.1.near, f32[5,12,32,128]{3,2,1,0:T(8,128)S(1)} %get-tuple-element.24.rim, ...), custom_call_target="tpu_custom_call" | custom-call | tf_op jit(solution)/shard_map/pallas_call | solution.py:414
  19.9 2.2 %collective-permute-start.2 = (f32[30,128]{1,0:T(8,128)S(1)}, f32[30,128]{1,0:T(8,128)S(1)}, u32[]{:S(2)}, u32[]{:S(2)}) collective-permute-start(f32[30,128]{1,0:T(8,128)S(1)} %get-tuple-element.30), channel_id=1, source_target_pairs={{1,2},{3,4},{5,6},{7,0},{2,1},{4,3},{6,5},{0,7},{9,10},{11,12},{13... | collective-permute-start | bytes 46088 | tf_op jit(solution)/shard_map/ppermute | solution.py:432
  22.1 0.0 collective-permute-start.3
  22.1 0.0 collective-permute-done.4.far
  22.1 0.0 collective-permute-done.5.near
  22.2 1.8 %shard_map.62 = (f32[5,512,128]{2,1,0:T(8,128)S(1)}, f32[5,256,128]{2,1,0:T(8,128)S(1)}, f32[5,2,8,128]{3,2,1,0:T(8,128)S(1)}) custom-call(f32[5,512,128]{2,1,0:T(8,128)S(1)} %get-tuple-element.27.own, f32[60,128]{1,0:T(8,128)S(1)} %collective-permute-done.4.far, f32[60,128]{1,0:T(8,128)S(1)} %collective-permute-done.5.near, ...), custom_call_target="tpu_custom_call" | custom-call | tf_op jit(solution)/shard_map/pallas_call | solution.py:414
  24.0 1.0 %collective-permute-done.2.far = f32[30,128]{1,0:T(8,128)S(1)} collective-permute-done((f32[30,128]{1,0:T(8,128)S(1)}, f32[30,128]{1,0:T(8,128)S(1)}, u32[]{:S(2)}, u32[]{:S(2)}) %collective-permute-start.2) | collective-permute-done | bytes 15392 | tf_op jit(solution)/shard_map/ppermute | solution.py:432
  24.9 0.0 collective-permute-done.3.near
  24.9 1.7 %shard_map.63 = (f32[768,128]{1,0:T(8,128)}, f32[3,768,128]{2,1,0:T(8,128)}, f32[768,128]{1,0:T(8,128)}) custom-call(f32[5,256,128]{2,1,0:T(8,128)S(1)} %get-tuple-element.29.edges.own, f32[30,128]{1,0:T(8,128)S(1)} %collective-permute-done.2.far, f32[30,128]{1,0:T(8,128)S(1)} %collective-permute-done.3.near, f32[5,256,128]{2,1,0:T(8,128)S(1)} %get-tuple-element.35.middle, ...), custom_call_target="tpu_custom_call" | custom-call | tf_op jit(solution)/shard_map/pallas_call | solution.py:414
Async XLA Ops:
  0.6 6.1 %copy-start.1 = (f32[32,24,128]{2,1,0:T(8,128)S(1)}, f32[32,24,128]{2,1,0:T(8,128)}, u32[]{:S(2)}) copy-start(f32[32,24,128]{2,1,0:T(8,128)} %density.3) | copy-start | bytes 1179652
  0.6 6.1 %copy-start = (f32[3,32,24,128]{3,2,1,0:T(8,128)S(1)}, f32[3,32,24,128]{3,2,1,0:T(8,128)}, u32[]{:S(2)}) copy-start(f32[3,32,24,128]{3,2,1,0:T(8,128)} %momentum.3) | copy-start | bytes 3538948
  0.7 6.1 %copy-start.2 = (f32[32,24,128]{2,1,0:T(8,128)S(1)}, f32[32,24,128]{2,1,0:T(8,128)}, u32[]{:S(2)}) copy-start(f32[32,24,128]{2,1,0:T(8,128)} %energy.3) | copy-start | bytes 1179652
  2.3 14.8 %collective-permute-start = (f32[5,3,32,128]{3,2,1,0:T(8,128)S(1)}, f32[5,3,32,128]{3,2,1,0:T(8,128)S(1)}, u32[]{:S(2)}, u32[]{:S(2)}) collective-permute-start(f32[5,3,32,128]{3,2,1,0:T(8,128)S(1)} %get-tuple-element.22), channel_id=1, source_target_pairs={{8,16},{24,0},{16,8},{0,24},{9,17},{25,1},{17,9},{1,25},{10,18},{2... | collective-permute-start | bytes 737288 | tf_op jit(solution)/shard_map/ppermute | solution.py:432
  6.2 11.5 %collective-permute-start.1 = (f32[5,3,32,128]{3,2,1,0:T(8,128)S(1)}, f32[5,3,32,128]{3,2,1,0:T(8,128)S(1)}, u32[]{:S(2)}, u32[]{:S(2)}) collective-permute-start(f32[5,3,32,128]{3,2,1,0:T(8,128)S(1)} %get-tuple-element.23), channel_id=1, source_target_pairs={{0,8},{16,24},{8,0},{24,16},{1,9},{17,25},{9,1},{25,17},{2,10},{18... | collective-permute-start | bytes 737288 | tf_op jit(solution)/shard_map/ppermute | solution.py:432
  12.8 9.4 %collective-permute-start.4 = (f32[60,128]{1,0:T(8,128)S(1)}, f32[60,128]{1,0:T(8,128)S(1)}, u32[]{:S(2)}, u32[]{:S(2)}) collective-permute-start(f32[60,128]{1,0:T(8,128)S(1)} %get-tuple-element.32), channel_id=1, source_target_pairs={{1,2},{3,4},{5,6},{7,0},{2,1},{4,3},{6,5},{0,7},{9,10},{11,12},{13... | collective-permute-start | bytes 92168 | tf_op jit(solution)/shard_map/ppermute | solution.py:432
  15.3 6.8 %collective-permute-start.5 = (f32[60,128]{1,0:T(8,128)S(1)}, f32[60,128]{1,0:T(8,128)S(1)}, u32[]{:S(2)}, u32[]{:S(2)}) collective-permute-start(f32[60,128]{1,0:T(8,128)S(1)} %get-tuple-element.33), channel_id=1, source_target_pairs={{0,1},{2,3},{4,5},{6,7},{1,0},{3,2},{5,4},{7,6},{8,9},{10,11},{12,... | collective-permute-start | bytes 92168 | tf_op jit(solution)/shard_map/ppermute | solution.py:432
  19.9 5.0 %collective-permute-start.2 = (f32[30,128]{1,0:T(8,128)S(1)}, f32[30,128]{1,0:T(8,128)S(1)}, u32[]{:S(2)}, u32[]{:S(2)}) collective-permute-start(f32[30,128]{1,0:T(8,128)S(1)} %get-tuple-element.30), channel_id=1, source_target_pairs={{1,2},{3,4},{5,6},{7,0},{2,1},{4,3},{6,5},{0,7},{9,10},{11,12},{13... | collective-permute-start | bytes 46088 | tf_op jit(solution)/shard_map/ppermute | solution.py:432
  22.1 2.8 %collective-permute-start.3 = (f32[30,128]{1,0:T(8,128)S(1)}, f32[30,128]{1,0:T(8,128)S(1)}, u32[]{:S(2)}, u32[]{:S(2)}) collective-permute-start(f32[30,128]{1,0:T(8,128)S(1)} %get-tuple-element.31), channel_id=1, source_target_pairs={{0,1},{2,3},{4,5},{6,7},{1,0},{3,2},{5,4},{7,6},{8,9},{10,11},{12,... | collective-permute-start | bytes 46088 | tf_op jit(solution)/shard_map/ppermute | solution.py:432

commit v6 on v5

--- a/solution.py
+++ b/solution.py
@@ -320,9 +320,7 @@
     deep = lanes // nx
     ahead, behind = shifts(0, nx)
     for side, source in enumerate(sides_of("gy", far, near)):
-
-        @pl.loop(0, halo)
-        def _(r):
+        for r in range(halo):
             fields = [source[f, r] for f in range(5)]
             flux = rolled(fields, ahead, behind, 0)
             for f in range(5):

time: 26.8 us -> 26.8 us (level)
  no operation moved by 1% of the time
where the time goes in v6:
time: 26.8 us; the launch traced here: 26.6 us
  Pallas kernels  15.1 us (56%)
  starting transfers between devices  9.28 us (35%)
  waiting for transfers between devices  1.56 us (6%)
  between operations  0.7 us (3%)
    pallas_call x5, Pallas kernels, call(): pl.pallas_call(kernel, out_shape=[jax.ShapeDtypeStruct(shape, jnp.float32...  13.4 us
    ppermute x3, starting transfers between devices, exchange(): lax.ppermute(far, axis, pairs[0])  8.74 us
    pallas_call x1, Pallas kernels, y_rows(): pl.pallas_call(rows_kernel, out_shape=[pltpu.VMEM(shape, jnp.float32)] *...  1.61 us
    ppermute x3, waiting for transfers between devices, exchange(): lax.ppermute(far, axis, pairs[0])  0.96 us
    ppermute x3, waiting for transfers between devices, exchange(): lax.ppermute(near, axis, pairs[1])  0.6 us
    ppermute x3, starting transfers between devices, exchange(): lax.ppermute(near, axis, pairs[1])  0.54 us
  transfers between devices with their start and end apart: 6, of which 2 were waited for; matrix products, arithmetic and copies ran while one was open for 0% of the time, Pallas kernels for 44%

profile of v6, /device:TPU:0, one launch (start us, length us, event | category | flops | bytes accessed | tf_op | source)
XLA Modules:
  0.0 26.6 jit_solution(2123709678455935042)
XLA Ops:
  0.6 0.0 copy-start.1
  0.6 0.0 copy-start
  0.7 0.0 copy-start.2
  0.7 1.6 %shard_map.58 = (f32[5,3,32,128]{3,2,1,0:T(8,128)S(1)}, f32[5,3,32,128]{3,2,1,0:T(8,128)S(1)}) custom-call(f32[32,24,128]{2,1,0:T(8,128)} %density.3, f32[3,32,24,128]{3,2,1,0:T(8,128)} %momentum.3, f32[32,24,128]{2,1,0:T(8,128)} %energy.3), custom_call_target="tpu_custom_call" | custom-call | tf_op jit(solution)/shard_map/pallas_call | solution.py:436
  2.3 4.0 %collective-permute-start = (f32[5,3,32,128]{3,2,1,0:T(8,128)S(1)}, f32[5,3,32,128]{3,2,1,0:T(8,128)S(1)}, u32[]{:S(2)}, u32[]{:S(2)}) collective-permute-start(f32[5,3,32,128]{3,2,1,0:T(8,128)S(1)} %get-tuple-element.22), channel_id=1, source_target_pairs={{8,16},{24,0},{16,8},{0,24},{9,17},{25,1},{17,9},{1,25},{10,18},{2... | collective-permute-start | bytes 737288 | tf_op jit(solution)/shard_map/ppermute | solution.py:430
  6.2 0.5 %collective-permute-start.1 = (f32[5,3,32,128]{3,2,1,0:T(8,128)S(1)}, f32[5,3,32,128]{3,2,1,0:T(8,128)S(1)}, u32[]{:S(2)}, u32[]{:S(2)}) collective-permute-start(f32[5,3,32,128]{3,2,1,0:T(8,128)S(1)} %get-tuple-element.23), channel_id=1, source_target_pairs={{0,8},{16,24},{8,0},{24,16},{1,9},{17,25},{9,1},{25,17},{2,10},{18... | collective-permute-start | bytes 737288 | tf_op jit(solution)/shard_map/ppermute | solution.py:430
  6.8 0.0 copy-done.1
  6.8 0.0 copy-done
  6.8 0.0 copy-done.2
  6.8 6.0 %shard_map.59 = (f32[5,512,128]{2,1,0:T(8,128)S(1)}, f32[60,128]{1,0:T(8,128)S(1)}, f32[60,128]{1,0:T(8,128)S(1)}, f32[5,12,32,128]{3,2,1,0:T(8,128)S(1)}, f32[5...) custom-call(f32[32,24,128]{2,1,0:T(8,128)S(1)} %copy-done.1, f32[3,32,24,128]{3,2,1,0:T(8,128)S(1)} %copy-done, ...), custom_call_target="tpu_custom_call" | custom-call | tf_op jit(solution)/shard_map/pallas_call | solution.py:412
  12.8 2.5 %collective-permute-start.4 = (f32[60,128]{1,0:T(8,128)S(1)}, f32[60,128]{1,0:T(8,128)S(1)}, u32[]{:S(2)}, u32[]{:S(2)}) collective-permute-start(f32[60,128]{1,0:T(8,128)S(1)} %get-tuple-element.32), channel_id=1, source_target_pairs={{1,2},{3,4},{5,6},{7,0},{2,1},{4,3},{6,5},{0,7},{9,10},{11,12},{13... | collective-permute-start | bytes 92168 | tf_op jit(solution)/shard_map/ppermute | solution.py:430
  15.3 0.0 collective-permute-start.5
  15.3 1.8 %shard_map.60 = (f32[5,512,128]{2,1,0:T(8,128)S(1)}, f32[5,2,16,128]{3,2,1,0:T(8,128)S(1)}) custom-call(f32[5,512,128]{2,1,0:T(8,128)S(1)} %get-tuple-element.27.own), custom_call_target="tpu_custom_call" | custom-call | tf_op jit(solution)/shard_map/pallas_call | solution.py:412
  17.1 0.0 collective-permute-done.far
  17.1 0.6 %collective-permute-done.1.near = f32[5,3,32,128]{3,2,1,0:T(8,128)S(1)} collective-permute-done((f32[5,3,32,128]{3,2,1,0:T(8,128)S(1)}, f32[5,3,32,128]{3,2,1,0:T(8,128)S(1)}, u32[]{:S(2)}, u32[]{:S(2)}) %collective-permute-start.1) | collective-permute-done | bytes 245792 | tf_op jit(solution)/shard_map/ppermute | solution.py:430
  17.7 2.2 %shard_map.61 = (f32[5,256,128]{2,1,0:T(8,128)S(1)}, f32[30,128]{1,0:T(8,128)S(1)}, f32[30,128]{1,0:T(8,128)S(1)}) custom-call(f32[5,3,32,128]{3,2,1,0:T(8,128)S(1)} %collective-permute-done.far, f32[5,3,32,128]{3,2,1,0:T(8,128)S(1)} %collective-permute-done.1.near, f32[5,12,32,128]{3,2,1,0:T(8,128)S(1)} %get-tuple-element.24.rim, ...), custom_call_target="tpu_custom_call" | custom-call | tf_op jit(solution)/shard_map/pallas_call | solution.py:412
  19.9 2.2 %collective-permute-start.2 = (f32[30,128]{1,0:T(8,128)S(1)}, f32[30,128]{1,0:T(8,128)S(1)}, u32[]{:S(2)}, u32[]{:S(2)}) collective-permute-start(f32[30,128]{1,0:T(8,128)S(1)} %get-tuple-element.30), channel_id=1, source_target_pairs={{1,2},{3,4},{5,6},{7,0},{2,1},{4,3},{6,5},{0,7},{9,10},{11,12},{13... | collective-permute-start | bytes 46088 | tf_op jit(solution)/shard_map/ppermute | solution.py:430
  22.1 0.0 collective-permute-start.3
  22.1 0.0 collective-permute-done.4.far
  22.1 0.0 collective-permute-done.5.near
  22.1 1.8 %shard_map.62 = (f32[5,512,128]{2,1,0:T(8,128)S(1)}, f32[5,256,128]{2,1,0:T(8,128)S(1)}, f32[5,2,8,128]{3,2,1,0:T(8,128)S(1)}) custom-call(f32[5,512,128]{2,1,0:T(8,128)S(1)} %get-tuple-element.27.own, f32[60,128]{1,0:T(8,128)S(1)} %collective-permute-done.4.far, f32[60,128]{1,0:T(8,128)S(1)} %collective-permute-done.5.near, ...), custom_call_target="tpu_custom_call" | custom-call | tf_op jit(solution)/shard_map/pallas_call | solution.py:412
  24.0 1.0 %collective-permute-done.2.far = f32[30,128]{1,0:T(8,128)S(1)} collective-permute-done((f32[30,128]{1,0:T(8,128)S(1)}, f32[30,128]{1,0:T(8,128)S(1)}, u32[]{:S(2)}, u32[]{:S(2)}) %collective-permute-start.2) | collective-permute-done | bytes 15392 | tf_op jit(solution)/shard_map/ppermute | solution.py:430
  24.9 0.0 collective-permute-done.3.near
  24.9 1.7 %shard_map.63 = (f32[768,128]{1,0:T(8,128)}, f32[3,768,128]{2,1,0:T(8,128)}, f32[768,128]{1,0:T(8,128)}) custom-call(f32[5,256,128]{2,1,0:T(8,128)S(1)} %get-tuple-element.29.edges.own, f32[30,128]{1,0:T(8,128)S(1)} %collective-permute-done.2.far, f32[30,128]{1,0:T(8,128)S(1)} %collective-permute-done.3.near, f32[5,256,128]{2,1,0:T(8,128)S(1)} %get-tuple-element.35.middle, ...), custom_call_target="tpu_custom_call" | custom-call | tf_op jit(solution)/shard_map/pallas_call | solution.py:412
Async XLA Ops:
  0.6 6.1 %copy-start.1 = (f32[32,24,128]{2,1,0:T(8,128)S(1)}, f32[32,24,128]{2,1,0:T(8,128)}, u32[]{:S(2)}) copy-start(f32[32,24,128]{2,1,0:T(8,128)} %density.3) | copy-start | bytes 1179652
  0.6 6.1 %copy-start = (f32[3,32,24,128]{3,2,1,0:T(8,128)S(1)}, f32[3,32,24,128]{3,2,1,0:T(8,128)}, u32[]{:S(2)}) copy-start(f32[3,32,24,128]{3,2,1,0:T(8,128)} %momentum.3) | copy-start | bytes 3538948
  0.7 6.1 %copy-start.2 = (f32[32,24,128]{2,1,0:T(8,128)S(1)}, f32[32,24,128]{2,1,0:T(8,128)}, u32[]{:S(2)}) copy-start(f32[32,24,128]{2,1,0:T(8,128)} %energy.3) | copy-start | bytes 1179652
  2.3 14.8 %collective-permute-start = (f32[5,3,32,128]{3,2,1,0:T(8,128)S(1)}, f32[5,3,32,128]{3,2,1,0:T(8,128)S(1)}, u32[]{:S(2)}, u32[]{:S(2)}) collective-permute-start(f32[5,3,32,128]{3,2,1,0:T(8,128)S(1)} %get-tuple-element.22), channel_id=1, source_target_pairs={{8,16},{24,0},{16,8},{0,24},{9,17},{25,1},{17,9},{1,25},{10,18},{2... | collective-permute-start | bytes 737288 | tf_op jit(solution)/shard_map/ppermute | solution.py:430
  6.2 11.5 %collective-permute-start.1 = (f32[5,3,32,128]{3,2,1,0:T(8,128)S(1)}, f32[5,3,32,128]{3,2,1,0:T(8,128)S(1)}, u32[]{:S(2)}, u32[]{:S(2)}) collective-permute-start(f32[5,3,32,128]{3,2,1,0:T(8,128)S(1)} %get-tuple-element.23), channel_id=1, source_target_pairs={{0,8},{16,24},{8,0},{24,16},{1,9},{17,25},{9,1},{25,17},{2,10},{18... | collective-permute-start | bytes 737288 | tf_op jit(solution)/shard_map/ppermute | solution.py:430
  12.8 9.4 %collective-permute-start.4 = (f32[60,128]{1,0:T(8,128)S(1)}, f32[60,128]{1,0:T(8,128)S(1)}, u32[]{:S(2)}, u32[]{:S(2)}) collective-permute-start(f32[60,128]{1,0:T(8,128)S(1)} %get-tuple-element.32), channel_id=1, source_target_pairs={{1,2},{3,4},{5,6},{7,0},{2,1},{4,3},{6,5},{0,7},{9,10},{11,12},{13... | collective-permute-start | bytes 92168 | tf_op jit(solution)/shard_map/ppermute | solution.py:430
  15.3 6.8 %collective-permute-start.5 = (f32[60,128]{1,0:T(8,128)S(1)}, f32[60,128]{1,0:T(8,128)S(1)}, u32[]{:S(2)}, u32[]{:S(2)}) collective-permute-start(f32[60,128]{1,0:T(8,128)S(1)} %get-tuple-element.33), channel_id=1, source_target_pairs={{0,1},{2,3},{4,5},{6,7},{1,0},{3,2},{5,4},{7,6},{8,9},{10,11},{12,... | collective-permute-start | bytes 92168 | tf_op jit(solution)/shard_map/ppermute | solution.py:430
  19.9 5.0 %collective-permute-start.2 = (f32[30,128]{1,0:T(8,128)S(1)}, f32[30,128]{1,0:T(8,128)S(1)}, u32[]{:S(2)}, u32[]{:S(2)}) collective-permute-start(f32[30,128]{1,0:T(8,128)S(1)} %get-tuple-element.30), channel_id=1, source_target_pairs={{1,2},{3,4},{5,6},{7,0},{2,1},{4,3},{6,5},{0,7},{9,10},{11,12},{13... | collective-permute-start | bytes 46088 | tf_op jit(solution)/shard_map/ppermute | solution.py:430
  22.1 2.8 %collective-permute-start.3 = (f32[30,128]{1,0:T(8,128)S(1)}, f32[30,128]{1,0:T(8,128)S(1)}, u32[]{:S(2)}, u32[]{:S(2)}) collective-permute-start(f32[30,128]{1,0:T(8,128)S(1)} %get-tuple-element.31), channel_id=1, source_target_pairs={{0,1},{2,3},{4,5},{6,7},{1,0},{3,2},{5,4},{7,6},{8,9},{10,11},{12,... | collective-permute-start | bytes 46088 | tf_op jit(solution)/shard_map/ppermute | solution.py:430

commit v7 on v5

--- a/solution.py
+++ b/solution.py
@@ -370,53 +370,75 @@
         pass
 
 
-def ends_kernel(count, own, far, near, middle, joint, edges, inner, edges_middle, edges_joint, swept):
+def ends_kernel(count, own, far, near, middle, joint, edges, inner, edges_middle, edges_joint, density, momentum, energy, swept, whole, sent):
     lanes = own.shape[-1]
+    nx, ny, _ = density.shape
+    deep = lanes // nx
+    outs = fields_of(density, momentum, energy)
     z_ends(own, far, near, middle, joint, swept, count)
+    copies = [pltpu.make_async_copy(whole.at[f], outs[f].at[:, pl.ds(8, ny - 16), :], sent.at[f]) for f in range(5)]
 
     def store(f, b, block):
         inner[f, pl.ds(b * lanes, lanes), :] = block
+        flat = whole.at[f].reshape(nx * (ny - 16), lanes)
+        for y in range(8, ny - 8):
+            at = (y - deep) * 8
+            flat[pl.ds(b * 8 * (ny - 16) + y - 8, 8, stride=ny - 16), :] = block[at : at + 8]
+
+    def turns():
+        for f in range(5):
+            yield from turn_out(swept, count, f, store)
+            copies[f].start()
 
     cells = edges.shape[1] // (quarters * 2) - 2 * halo
-    turns = (None for f in range(5) for _ in turn_out(swept, count, f, store))
-    alternate(z_middle(edges, edges_middle, edges_joint, 2), cells, turns, 5 * count)
-
-
-def last_kernel(ny, own, far, near, middle, joint, inner, density, momentum, energy, swept, whole, sent):
+    alternate(z_middle(edges, edges_middle, edges_joint, 2), cells // 2, turns(), 5 * count)
+    for copy in copies:
+        copy.wait()
+
+
+def last_kernel(own, far, near, middle, joint, inner, _, __, ___, density, momentum, energy, swept, whole, sent):
     lanes = own.shape[-1]
-    nx = density.shape[0] // ny
+    nx, ny, _ = density.shape
     deep = lanes // nx
     strip = 2 * deep * 8
     outs = fields_of(density, momentum, energy)
     z_ends(own, far, near, middle, joint, swept, 2)
 
+    def put(f, x, y, value):
+        flat = whole.at[f, int(y >= 8)].reshape(nx * 8, lanes)
+        flat[pl.ds(x * 8 + y % 8, 8, stride=8), :] = value
+
     def store(f, b, block):
         for half in range(lanes // strip):
             for k in range(2 * deep):
-                y = k if k < deep else ny - 2 * deep + k
                 at = half * strip + k * 8
-                whole[f, pl.ds((b * (lanes // strip) + half) * 8 * ny + y, 8, stride=ny), :] = block[at : at + 8]
-
-    copies = [pltpu.make_async_copy(whole.at[f], outs[f], sent.at[f]) for f in range(5)]
+                put(f, (b * (lanes // strip) + half) * 8, k if k < deep else ny - 2 * deep + k, block[at : at + 8])
+
     for f in range(5):
         for b in range(nx // 8):
-            for i in range(deep, ny - deep):
-                whole[f, pl.ds(b * 8 * ny + i, 8, stride=ny), :] = inner[f, row(b * lanes + (i - deep) * 8), :]
+            for y in [*range(deep, 8), *range(ny - 8, ny - deep)]:
+                put(f, b * 8, y, inner[f, row(b * lanes + (y - deep) * 8), :])
+    copies = []
+    for f in range(5):
         for _ in turn_out(swept, 2, f, store):
             pass
-        copies[f].start()
+        for side in range(2):
+            rows = outs[f].at[:, pl.ds(side * (ny - 8), 8), :]
+            copies.append(pltpu.make_async_copy(whole.at[f, side], rows, sent.at[f, side]))
+            copies[-1].start()
     for copy in copies:
         copy.wait()
 
 
-def call(kernel, shapes, scratch, arguments, in_specs=None, out_spec=None):
+def call(kernel, shapes, scratch, arguments, in_specs=None, out_specs=None, aliases=None):
     whole = pl.BlockSpec(memory_space=pltpu.VMEM)
     return pl.pallas_call(
         kernel,
         out_shape=[jax.ShapeDtypeStruct(shape, jnp.float32) for shape in shapes],
         in_specs=[whole] * len(arguments) if in_specs is None else in_specs,
-        out_specs=[whole if out_spec is None else out_spec] * len(shapes),
+        out_specs=[whole] * len(shapes) if out_specs is None else out_specs,
         scratch_shapes=[pltpu.VMEM(a, jnp.float32) if isinstance(a, tuple) else a for a in scratch],
+        input_output_aliases=aliases or {},
         compiler_params=pltpu.CompilerParams(vmem_limit_bytes=24 * 2**20),
     )(*arguments)
 
@@ -474,21 +496,24 @@
         [whole] * 5 + [anywhere],
     )
     far_edges, near_edges = exchange("gz", far_edges, near_edges)
-    inner, edges_middle, edges_faces = call(
+    results = [(nx, ny, nz), (3, nx, ny, nz), (nx, ny, nz)]
+    inner, edges_middle, edges_faces, *outs = call(
         functools.partial(ends_kernel, count),
-        [(5, count * nz, nz), (5, 2 * nz, nz), (5, 2, quarters * 2, nz)],
-        [(5, count * nz, nz)],
+        [(5, count * nz, nz), (5, 2 * nz, nz), (5, 2, quarters * 2, nz)] + results,
+        [(5, count * nz, nz), (5, nx, ny - 16, nz), pltpu.SemaphoreType.DMA((5,))],
         [turned, far, near, middle, faces, edges],
-    )
-    cells = nx * ny
+        out_specs=[whole] * 3 + [anywhere] * 3,
+    )
     outs = call(
-        functools.partial(last_kernel, ny),
-        [(cells, nz), (3, cells, nz), (cells, nz)],
-        [(5, 2 * nz, nz), (5, cells, nz), pltpu.SemaphoreType.DMA((5,))],
-        [edges, far_edges, near_edges, edges_middle, edges_faces, inner],
-        out_spec=anywhere,
-    )
-    return (outs[0].reshape(nx, ny, nz), outs[1].reshape(3, nx, ny, nz), outs[2].reshape(nx, ny, nz))
+        last_kernel,
+        results,
+        [(5, 2 * nz, nz), (5, 2, nx, 8, nz), pltpu.SemaphoreType.DMA((5, 2))],
+        [edges, far_edges, near_edges, edges_middle, edges_faces, inner, *outs],
+        [whole] * 6 + [anywhere] * 3,
+        [anywhere] * 3,
+        {6: 0, 7: 1, 8: 2},
+    )
+    return tuple(outs)
 
 
 def solution(mesh):

time: 26.8 us -> 26.6 us (level)
  transfers between devices with their start and end apart: 6 -> 6, of which waited for: 2 -> 2; matrix products, arithmetic and copies ran while one was open for 0% -> 0% of each run, Pallas kernels for 44% -> 45%
where the time goes in v7:
time: 26.6 us; the launch traced here: 26.5 us
  Pallas kernels  15.2 us (57%)
  starting transfers between devices  9.28 us (35%)
  waiting for transfers between devices  1.32 us (5%)
  between operations  0.7 us (3%)
    pallas_call x5, Pallas kernels, call(): pl.pallas_call(kernel, out_shape=[jax.ShapeDtypeStruct(shape, jnp.float32...  13.6 us
    ppermute x3, starting transfers between devices, exchange(): lax.ppermute(far, axis, pairs[0])  8.74 us
    pallas_call x1, Pallas kernels, y_rows(): pl.pallas_call(rows_kernel, out_shape=[pltpu.VMEM(shape, jnp.float32)] *...  1.61 us
    ppermute x3, waiting for transfers between devices, exchange(): lax.ppermute(far, axis, pairs[0])  0.72 us
    ppermute x3, waiting for transfers between devices, exchange(): lax.ppermute(near, axis, pairs[1])  0.6 us
    ppermute x3, starting transfers between devices, exchange(): lax.ppermute(near, axis, pairs[1])  0.54 us
  transfers between devices with their start and end apart: 6, of which 2 were waited for; matrix products, arithmetic and copies ran while one was open for 0% of the time, Pallas kernels for 45%

profile of v7, /device:TPU:0, one launch (start us, length us, event | category | flops | bytes accessed | tf_op | source)
XLA Modules:
  0.0 26.5 jit_solution(1876604050244127330)
XLA Ops:
  0.6 0.0 copy-start.2
  0.6 0.0 copy-start
  0.7 0.0 copy-start.1
  0.7 1.6 %shard_map.58 = (f32[5,3,32,128]{3,2,1,0:T(8,128)S(1)}, f32[5,3,32,128]{3,2,1,0:T(8,128)S(1)}) custom-call(f32[32,24,128]{2,1,0:T(8,128)} %density.3, f32[3,32,24,128]{3,2,1,0:T(8,128)} %momentum.3, f32[32,24,128]{2,1,0:T(8,128)} %energy.3), custom_call_target="tpu_custom_call" | custom-call | tf_op jit(solution)/shard_map/pallas_call | solution.py:460
  2.3 4.0 %collective-permute-start = (f32[5,3,32,128]{3,2,1,0:T(8,128)S(1)}, f32[5,3,32,128]{3,2,1,0:T(8,128)S(1)}, u32[]{:S(2)}, u32[]{:S(2)}) collective-permute-start(f32[5,3,32,128]{3,2,1,0:T(8,128)S(1)} %get-tuple-element.22), channel_id=1, source_target_pairs={{8,16},{24,0},{16,8},{0,24},{9,17},{25,1},{17,9},{1,25},{10,18},{2... | collective-permute-start | bytes 737288 | tf_op jit(solution)/shard_map/ppermute | solution.py:454
  6.2 0.5 %collective-permute-start.1 = (f32[5,3,32,128]{3,2,1,0:T(8,128)S(1)}, f32[5,3,32,128]{3,2,1,0:T(8,128)S(1)}, u32[]{:S(2)}, u32[]{:S(2)}) collective-permute-start(f32[5,3,32,128]{3,2,1,0:T(8,128)S(1)} %get-tuple-element.23), channel_id=1, source_target_pairs={{0,8},{16,24},{8,0},{24,16},{1,9},{17,25},{9,1},{25,17},{2,10},{18... | collective-permute-start | bytes 737288 | tf_op jit(solution)/shard_map/ppermute | solution.py:454
  6.8 0.0 copy-done.2
  6.8 0.0 copy-done
  6.8 0.0 copy-done.1
  6.8 6.0 %shard_map.59 = (f32[5,512,128]{2,1,0:T(8,128)S(1)}, f32[60,128]{1,0:T(8,128)S(1)}, f32[60,128]{1,0:T(8,128)S(1)}, f32[5,12,32,128]{3,2,1,0:T(8,128)S(1)}, f32[5...) custom-call(f32[32,24,128]{2,1,0:T(8,128)S(1)} %copy-done.1, f32[3,32,24,128]{3,2,1,0:T(8,128)S(1)} %copy-done, ...), custom_call_target="tpu_custom_call" | custom-call | tf_op jit(solution)/shard_map/pallas_call | solution.py:435
  12.8 2.5 %collective-permute-start.4 = (f32[60,128]{1,0:T(8,128)S(1)}, f32[60,128]{1,0:T(8,128)S(1)}, u32[]{:S(2)}, u32[]{:S(2)}) collective-permute-start(f32[60,128]{1,0:T(8,128)S(1)} %get-tuple-element.32), channel_id=1, source_target_pairs={{1,2},{3,4},{5,6},{7,0},{2,1},{4,3},{6,5},{0,7},{9,10},{11,12},{13... | collective-permute-start | bytes 92168 | tf_op jit(solution)/shard_map/ppermute | solution.py:454
  15.3 0.0 collective-permute-start.5
  15.3 1.8 %shard_map.60 = (f32[5,512,128]{2,1,0:T(8,128)S(1)}, f32[5,2,16,128]{3,2,1,0:T(8,128)S(1)}) custom-call(f32[5,512,128]{2,1,0:T(8,128)S(1)} %get-tuple-element.27.own), custom_call_target="tpu_custom_call" | custom-call | tf_op jit(solution)/shard_map/pallas_call | solution.py:435
  17.1 0.0 collective-permute-done.far
  17.1 0.6 %collective-permute-done.1.near = f32[5,3,32,128]{3,2,1,0:T(8,128)S(1)} collective-permute-done((f32[5,3,32,128]{3,2,1,0:T(8,128)S(1)}, f32[5,3,32,128]{3,2,1,0:T(8,128)S(1)}, u32[]{:S(2)}, u32[]{:S(2)}) %collective-permute-start.1) | collective-permute-done | bytes 245792 | tf_op jit(solution)/shard_map/ppermute | solution.py:454
  17.7 2.2 %shard_map.61 = (f32[5,256,128]{2,1,0:T(8,128)S(1)}, f32[30,128]{1,0:T(8,128)S(1)}, f32[30,128]{1,0:T(8,128)S(1)}) custom-call(f32[5,3,32,128]{3,2,1,0:T(8,128)S(1)} %collective-permute-done.far, f32[5,3,32,128]{3,2,1,0:T(8,128)S(1)} %collective-permute-done.1.near, f32[5,12,32,128]{3,2,1,0:T(8,128)S(1)} %get-tuple-element.24.rim, ...), custom_call_target="tpu_custom_call" | custom-call | tf_op jit(solution)/shard_map/pallas_call | solution.py:435
  19.9 2.2 %collective-permute-start.2 = (f32[30,128]{1,0:T(8,128)S(1)}, f32[30,128]{1,0:T(8,128)S(1)}, u32[]{:S(2)}, u32[]{:S(2)}) collective-permute-start(f32[30,128]{1,0:T(8,128)S(1)} %get-tuple-element.30), channel_id=1, source_target_pairs={{1,2},{3,4},{5,6},{7,0},{2,1},{4,3},{6,5},{0,7},{9,10},{11,12},{13... | collective-permute-start | bytes 46088 | tf_op jit(solution)/shard_map/ppermute | solution.py:454
  22.1 0.0 collective-permute-start.3
  22.1 0.0 collective-permute-done.4.far
  22.1 0.0 collective-permute-done.5.near
  22.2 2.1 %shard_map.62 = (f32[5,512,128]{2,1,0:T(8,128)S(1)}, f32[5,256,128]{2,1,0:T(8,128)S(1)}, f32[5,2,8,128]{3,2,1,0:T(8,128)S(1)}, f32[32,24,128]{2,1,0:T(8,128)}, f...) custom-call(f32[5,512,128]{2,1,0:T(8,128)S(1)} %get-tuple-element.27.own, f32[60,128]{1,0:T(8,128)S(1)} %collective-permute-done.4.far, ...), custom_call_target="tpu_custom_call" | custom-call | tf_op jit(solution)/shard_map/pallas_call | solution.py:435
  24.2 0.7 %collective-permute-done.2.far = f32[30,128]{1,0:T(8,128)S(1)} collective-permute-done((f32[30,128]{1,0:T(8,128)S(1)}, f32[30,128]{1,0:T(8,128)S(1)}, u32[]{:S(2)}, u32[]{:S(2)}) %collective-permute-start.2) | collective-permute-done | bytes 15392 | tf_op jit(solution)/shard_map/ppermute | solution.py:454
  24.9 0.0 collective-permute-done.3.near
  24.9 1.5 %shard_map.63 = (f32[32,24,128]{2,1,0:T(8,128)}, f32[3,32,24,128]{3,2,1,0:T(8,128)}, f32[32,24,128]{2,1,0:T(8,128)}) custom-call(f32[5,256,128]{2,1,0:T(8,128)S(1)} %get-tuple-element.29.edges.own, f32[30,128]{1,0:T(8,128)S(1)} %collective-permute-done.2.far, ...), custom_call_target="tpu_custom_call", output_to_operand_aliasing={{0}: (6, {}), {1}: (7, {}), {2}: (8, {})} | custom-call | tf_op jit(solution)/shard_map/pallas_call | solution.py:435
Async XLA Ops:
  0.6 6.1 %copy-start.2 = (f32[32,24,128]{2,1,0:T(8,128)S(1)}, f32[32,24,128]{2,1,0:T(8,128)}, u32[]{:S(2)}) copy-start(f32[32,24,128]{2,1,0:T(8,128)} %energy.3) | copy-start | bytes 1179652
  0.6 6.1 %copy-start = (f32[3,32,24,128]{3,2,1,0:T(8,128)S(1)}, f32[3,32,24,128]{3,2,1,0:T(8,128)}, u32[]{:S(2)}) copy-start(f32[3,32,24,128]{3,2,1,0:T(8,128)} %momentum.3) | copy-start | bytes 3538948
  0.7 6.1 %copy-start.1 = (f32[32,24,128]{2,1,0:T(8,128)S(1)}, f32[32,24,128]{2,1,0:T(8,128)}, u32[]{:S(2)}) copy-start(f32[32,24,128]{2,1,0:T(8,128)} %density.3) | copy-start | bytes 1179652
  2.3 14.8 %collective-permute-start = (f32[5,3,32,128]{3,2,1,0:T(8,128)S(1)}, f32[5,3,32,128]{3,2,1,0:T(8,128)S(1)}, u32[]{:S(2)}, u32[]{:S(2)}) collective-permute-start(f32[5,3,32,128]{3,2,1,0:T(8,128)S(1)} %get-tuple-element.22), channel_id=1, source_target_pairs={{8,16},{24,0},{16,8},{0,24},{9,17},{25,1},{17,9},{1,25},{10,18},{2... | collective-permute-start | bytes 737288 | tf_op jit(solution)/shard_map/ppermute | solution.py:454
  6.2 11.5 %collective-permute-start.1 = (f32[5,3,32,128]{3,2,1,0:T(8,128)S(1)}, f32[5,3,32,128]{3,2,1,0:T(8,128)S(1)}, u32[]{:S(2)}, u32[]{:S(2)}) collective-permute-start(f32[5,3,32,128]{3,2,1,0:T(8,128)S(1)} %get-tuple-element.23), channel_id=1, source_target_pairs={{0,8},{16,24},{8,0},{24,16},{1,9},{17,25},{9,1},{25,17},{2,10},{18... | collective-permute-start | bytes 737288 | tf_op jit(solution)/shard_map/ppermute | solution.py:454
  12.8 9.4 %collective-permute-start.4 = (f32[60,128]{1,0:T(8,128)S(1)}, f32[60,128]{1,0:T(8,128)S(1)}, u32[]{:S(2)}, u32[]{:S(2)}) collective-permute-start(f32[60,128]{1,0:T(8,128)S(1)} %get-tuple-element.32), channel_id=1, source_target_pairs={{1,2},{3,4},{5,6},{7,0},{2,1},{4,3},{6,5},{0,7},{9,10},{11,12},{13... | collective-permute-start | bytes 92168 | tf_op jit(solution)/shard_map/ppermute | solution.py:454
  15.3 6.8 %collective-permute-start.5 = (f32[60,128]{1,0:T(8,128)S(1)}, f32[60,128]{1,0:T(8,128)S(1)}, u32[]{:S(2)}, u32[]{:S(2)}) collective-permute-start(f32[60,128]{1,0:T(8,128)S(1)} %get-tuple-element.33), channel_id=1, source_target_pairs={{0,1},{2,3},{4,5},{6,7},{1,0},{3,2},{5,4},{7,6},{8,9},{10,11},{12,... | collective-permute-start | bytes 92168 | tf_op jit(solution)/shard_map/ppermute | solution.py:454
  19.9 5.0 %collective-permute-start.2 = (f32[30,128]{1,0:T(8,128)S(1)}, f32[30,128]{1,0:T(8,128)S(1)}, u32[]{:S(2)}, u32[]{:S(2)}) collective-permute-start(f32[30,128]{1,0:T(8,128)S(1)} %get-tuple-element.30), channel_id=1, source_target_pairs={{1,2},{3,4},{5,6},{7,0},{2,1},{4,3},{6,5},{0,7},{9,10},{11,12},{13... | collective-permute-start | bytes 46088 | tf_op jit(solution)/shard_map/ppermute | solution.py:454
  22.1 2.8 %collective-permute-start.3 = (f32[30,128]{1,0:T(8,128)S(1)}, f32[30,128]{1,0:T(8,128)S(1)}, u32[]{:S(2)}, u32[]{:S(2)}) collective-permute-start(f32[30,128]{1,0:T(8,128)S(1)} %get-tuple-element.31), channel_id=1, source_target_pairs={{0,1},{2,3},{4,5},{6,7},{1,0},{3,2},{5,4},{7,6},{8,9},{10,11},{12,... | collective-permute-start | bytes 46088 | tf_op jit(solution)/shard_map/ppermute | solution.py:454

commit v8 on v5

--- a/solution.py
+++ b/solution.py
@@ -314,7 +314,7 @@
     ends(turned, count, far, near)
 
 
-def edge_kernel(far, near, rim, beside, joint, _, turned, far_end, near_end, ghost, *outers):
+def edge_kernel(near, far, rim, beside, joint, _, turned, far_end, near_end, ghost, *outers):
     _, kept, nx, lanes = rim.shape
     kept = kept // 2
     deep = lanes // nx
@@ -470,7 +470,7 @@
         edge_kernel,
         [(5, 2 * nz, nz)] + [(5 * halo * 2, nz)] * 2,
         [(5, 2 * halo, nx, nz)] + [(5, nz, nz)] * 2,
-        [far_rows, near_rows, rim, beside, joint, faces],
+        [near_rows, far_rows, rim, beside, joint, faces],
         [whole] * 5 + [anywhere],
     )
     far_edges, near_edges = exchange("gz", far_edges, near_edges)

time: 26.8 us -> 26.8 us (level)
    ppermute x3, starting transfers between devices: 8.74 us -> 6.27 us  [exchange(): lax.ppermute(far, axis, pairs[0])]
    ppermute x3, starting transfers between devices: 0.54 us -> 3.01 us  [exchange(): lax.ppermute(near, axis, pairs[1])]
    ppermute x3, waiting for transfers between devices: 0.96 us -> 1.55 us  [exchange(): lax.ppermute(far, axis, pairs[0])]
    ppermute x3, waiting for transfers between devices: 0.6 us -> 0.01 us  [exchange(): lax.ppermute(near, axis, pairs[1])]
where the time goes in v8:
time: 26.8 us; the launch traced here: 26.6 us
  Pallas kernels  15.1 us (56%)
  starting transfers between devices  9.28 us (35%)
  waiting for transfers between devices  1.56 us (6%)
  between operations  0.7 us (3%)
    pallas_call x5, Pallas kernels, call(): pl.pallas_call(kernel, out_shape=[jax.ShapeDtypeStruct(shape, jnp.float32...  13.5 us
    ppermute x3, starting transfers between devices, exchange(): lax.ppermute(far, axis, pairs[0])  6.27 us
    ppermute x3, starting transfers between devices, exchange(): lax.ppermute(near, axis, pairs[1])  3.01 us
    pallas_call x1, Pallas kernels, y_rows(): pl.pallas_call(rows_kernel, out_shape=[pltpu.VMEM(shape, jnp.float32)] *...  1.61 us
    ppermute x3, waiting for transfers between devices, exchange(): lax.ppermute(far, axis, pairs[0])  1.55 us
  transfers between devices with their start and end apart: 6, of which 2 were waited for; matrix products, arithmetic and copies ran while one was open for 0% of the time, Pallas kernels for 44%

profile of v8, /device:TPU:0, one launch (start us, length us, event | category | flops | bytes accessed | tf_op | source)
XLA Modules:
  0.0 26.6 jit_solution(1656627554398537529)
XLA Ops:
  0.6 0.0 copy-start.1
  0.6 0.0 copy-start
  0.7 0.0 copy-start.2
  0.7 1.6 %shard_map.58 = (f32[5,3,32,128]{3,2,1,0:T(8,128)S(1)}, f32[5,3,32,128]{3,2,1,0:T(8,128)S(1)}) custom-call(f32[32,24,128]{2,1,0:T(8,128)} %density.3, f32[3,32,24,128]{3,2,1,0:T(8,128)} %momentum.3, f32[32,24,128]{2,1,0:T(8,128)} %energy.3), custom_call_target="tpu_custom_call" | custom-call | tf_op jit(solution)/shard_map/pallas_call | solution.py:438
  2.3 3.0 %collective-permute-start = (f32[5,3,32,128]{3,2,1,0:T(8,128)S(1)}, f32[5,3,32,128]{3,2,1,0:T(8,128)S(1)}, u32[]{:S(2)}, u32[]{:S(2)}) collective-permute-start(f32[5,3,32,128]{3,2,1,0:T(8,128)S(1)} %get-tuple-element.22), channel_id=1, source_target_pairs={{0,8},{16,24},{8,0},{24,16},{1,9},{17,25},{9,1},{25,17},{2,10},{18... | collective-permute-start | bytes 737288 | tf_op jit(solution)/shard_map/ppermute | solution.py:432
  5.3 1.5 %collective-permute-start.1 = (f32[5,3,32,128]{3,2,1,0:T(8,128)S(1)}, f32[5,3,32,128]{3,2,1,0:T(8,128)S(1)}, u32[]{:S(2)}, u32[]{:S(2)}) collective-permute-start(f32[5,3,32,128]{3,2,1,0:T(8,128)S(1)} %get-tuple-element.23), channel_id=1, source_target_pairs={{8,16},{24,0},{16,8},{0,24},{9,17},{25,1},{17,9},{1,25},{10,18},{2... | collective-permute-start | bytes 737288 | tf_op jit(solution)/shard_map/ppermute | solution.py:432
  6.8 0.0 copy-done.1
  6.8 0.0 copy-done
  6.8 0.0 copy-done.2
  6.8 6.0 %shard_map.59 = (f32[5,512,128]{2,1,0:T(8,128)S(1)}, f32[60,128]{1,0:T(8,128)S(1)}, f32[60,128]{1,0:T(8,128)S(1)}, f32[5,12,32,128]{3,2,1,0:T(8,128)S(1)}, f32[5...) custom-call(f32[32,24,128]{2,1,0:T(8,128)S(1)} %copy-done.1, f32[3,32,24,128]{3,2,1,0:T(8,128)S(1)} %copy-done, ...), custom_call_target="tpu_custom_call" | custom-call | tf_op jit(solution)/shard_map/pallas_call | solution.py:414
  12.8 2.5 %collective-permute-start.4 = (f32[60,128]{1,0:T(8,128)S(1)}, f32[60,128]{1,0:T(8,128)S(1)}, u32[]{:S(2)}, u32[]{:S(2)}) collective-permute-start(f32[60,128]{1,0:T(8,128)S(1)} %get-tuple-element.32), channel_id=1, source_target_pairs={{1,2},{3,4},{5,6},{7,0},{2,1},{4,3},{6,5},{0,7},{9,10},{11,12},{13... | collective-permute-start | bytes 92168 | tf_op jit(solution)/shard_map/ppermute | solution.py:432
  15.3 0.0 collective-permute-start.5
  15.3 1.8 %shard_map.60 = (f32[5,512,128]{2,1,0:T(8,128)S(1)}, f32[5,2,16,128]{3,2,1,0:T(8,128)S(1)}) custom-call(f32[5,512,128]{2,1,0:T(8,128)S(1)} %get-tuple-element.27.own), custom_call_target="tpu_custom_call" | custom-call | tf_op jit(solution)/shard_map/pallas_call | solution.py:414
  17.1 0.0 collective-permute-done.near
  17.1 0.6 %collective-permute-done.1.far = f32[5,3,32,128]{3,2,1,0:T(8,128)S(1)} collective-permute-done((f32[5,3,32,128]{3,2,1,0:T(8,128)S(1)}, f32[5,3,32,128]{3,2,1,0:T(8,128)S(1)}, u32[]{:S(2)}, u32[]{:S(2)}) %collective-permute-start.1) | collective-permute-done | bytes 245792 | tf_op jit(solution)/shard_map/ppermute | solution.py:432
  17.7 2.2 %shard_map.61 = (f32[5,256,128]{2,1,0:T(8,128)S(1)}, f32[30,128]{1,0:T(8,128)S(1)}, f32[30,128]{1,0:T(8,128)S(1)}) custom-call(f32[5,3,32,128]{3,2,1,0:T(8,128)S(1)} %collective-permute-done.near, f32[5,3,32,128]{3,2,1,0:T(8,128)S(1)} %collective-permute-done.1.far, f32[5,12,32,128]{3,2,1,0:T(8,128)S(1)} %get-tuple-element.24.rim, ...), custom_call_target="tpu_custom_call" | custom-call | tf_op jit(solution)/shard_map/pallas_call | solution.py:414
  19.9 2.2 %collective-permute-start.2 = (f32[30,128]{1,0:T(8,128)S(1)}, f32[30,128]{1,0:T(8,128)S(1)}, u32[]{:S(2)}, u32[]{:S(2)}) collective-permute-start(f32[30,128]{1,0:T(8,128)S(1)} %get-tuple-element.30), channel_id=1, source_target_pairs={{1,2},{3,4},{5,6},{7,0},{2,1},{4,3},{6,5},{0,7},{9,10},{11,12},{13... | collective-permute-start | bytes 46088 | tf_op jit(solution)/shard_map/ppermute | solution.py:432
  22.1 0.0 collective-permute-start.3
  22.1 0.0 collective-permute-done.4.far
  22.1 0.0 collective-permute-done.5.near
  22.2 1.8 %shard_map.62 = (f32[5,512,128]{2,1,0:T(8,128)S(1)}, f32[5,256,128]{2,1,0:T(8,128)S(1)}, f32[5,2,8,128]{3,2,1,0:T(8,128)S(1)}) custom-call(f32[5,512,128]{2,1,0:T(8,128)S(1)} %get-tuple-element.27.own, f32[60,128]{1,0:T(8,128)S(1)} %collective-permute-done.4.far, f32[60,128]{1,0:T(8,128)S(1)} %collective-permute-done.5.near, ...), custom_call_target="tpu_custom_call" | custom-call | tf_op jit(solution)/shard_map/pallas_call | solution.py:414
  24.0 1.0 %collective-permute-done.2.far = f32[30,128]{1,0:T(8,128)S(1)} collective-permute-done((f32[30,128]{1,0:T(8,128)S(1)}, f32[30,128]{1,0:T(8,128)S(1)}, u32[]{:S(2)}, u32[]{:S(2)}) %collective-permute-start.2) | collective-permute-done | bytes 15392 | tf_op jit(solution)/shard_map/ppermute | solution.py:432
  24.9 0.0 collective-permute-done.3.near
  24.9 1.7 %shard_map.63 = (f32[768,128]{1,0:T(8,128)}, f32[3,768,128]{2,1,0:T(8,128)}, f32[768,128]{1,0:T(8,128)}) custom-call(f32[5,256,128]{2,1,0:T(8,128)S(1)} %get-tuple-element.29.edges.own, f32[30,128]{1,0:T(8,128)S(1)} %collective-permute-done.2.far, f32[30,128]{1,0:T(8,128)S(1)} %collective-permute-done.3.near, f32[5,256,128]{2,1,0:T(8,128)S(1)} %get-tuple-element.35.middle, ...), custom_call_target="tpu_custom_call" | custom-call | tf_op jit(solution)/shard_map/pallas_call | solution.py:414
Async XLA Ops:
  0.6 6.1 %copy-start.1 = (f32[32,24,128]{2,1,0:T(8,128)S(1)}, f32[32,24,128]{2,1,0:T(8,128)}, u32[]{:S(2)}) copy-start(f32[32,24,128]{2,1,0:T(8,128)} %density.3) | copy-start | bytes 1179652
  0.6 6.1 %copy-start = (f32[3,32,24,128]{3,2,1,0:T(8,128)S(1)}, f32[3,32,24,128]{3,2,1,0:T(8,128)}, u32[]{:S(2)}) copy-start(f32[3,32,24,128]{3,2,1,0:T(8,128)} %momentum.3) | copy-start | bytes 3538948
  0.7 6.1 %copy-start.2 = (f32[32,24,128]{2,1,0:T(8,128)S(1)}, f32[32,24,128]{2,1,0:T(8,128)}, u32[]{:S(2)}) copy-start(f32[32,24,128]{2,1,0:T(8,128)} %energy.3) | copy-start | bytes 1179652
  2.3 14.8 %collective-permute-start = (f32[5,3,32,128]{3,2,1,0:T(8,128)S(1)}, f32[5,3,32,128]{3,2,1,0:T(8,128)S(1)}, u32[]{:S(2)}, u32[]{:S(2)}) collective-permute-start(f32[5,3,32,128]{3,2,1,0:T(8,128)S(1)} %get-tuple-element.22), channel_id=1, source_target_pairs={{0,8},{16,24},{8,0},{24,16},{1,9},{17,25},{9,1},{25,17},{2,10},{18... | collective-permute-start | bytes 737288 | tf_op jit(solution)/shard_map/ppermute | solution.py:432
  5.3 12.4 %collective-permute-start.1 = (f32[5,3,32,128]{3,2,1,0:T(8,128)S(1)}, f32[5,3,32,128]{3,2,1,0:T(8,128)S(1)}, u32[]{:S(2)}, u32[]{:S(2)}) collective-permute-start(f32[5,3,32,128]{3,2,1,0:T(8,128)S(1)} %get-tuple-element.23), channel_id=1, source_target_pairs={{8,16},{24,0},{16,8},{0,24},{9,17},{25,1},{17,9},{1,25},{10,18},{2... | collective-permute-start | bytes 737288 | tf_op jit(solution)/shard_map/ppermute | solution.py:432
  12.8 9.4 %collective-permute-start.4 = (f32[60,128]{1,0:T(8,128)S(1)}, f32[60,128]{1,0:T(8,128)S(1)}, u32[]{:S(2)}, u32[]{:S(2)}) collective-permute-start(f32[60,128]{1,0:T(8,128)S(1)} %get-tuple-element.32), channel_id=1, source_target_pairs={{1,2},{3,4},{5,6},{7,0},{2,1},{4,3},{6,5},{0,7},{9,10},{11,12},{13... | collective-permute-start | bytes 92168 | tf_op jit(solution)/shard_map/ppermute | solution.py:432
  15.3 6.8 %collective-permute-start.5 = (f32[60,128]{1,0:T(8,128)S(1)}, f32[60,128]{1,0:T(8,128)S(1)}, u32[]{:S(2)}, u32[]{:S(2)}) collective-permute-start(f32[60,128]{1,0:T(8,128)S(1)} %get-tuple-element.33), channel_id=1, source_target_pairs={{0,1},{2,3},{4,5},{6,7},{1,0},{3,2},{5,4},{7,6},{8,9},{10,11},{12,... | collective-permute-start | bytes 92168 | tf_op jit(solution)/shard_map/ppermute | solution.py:432
  19.9 5.0 %collective-permute-start.2 = (f32[30,128]{1,0:T(8,128)S(1)}, f32[30,128]{1,0:T(8,128)S(1)}, u32[]{:S(2)}, u32[]{:S(2)}) collective-permute-start(f32[30,128]{1,0:T(8,128)S(1)} %get-tuple-element.30), channel_id=1, source_target_pairs={{1,2},{3,4},{5,6},{7,0},{2,1},{4,3},{6,5},{0,7},{9,10},{11,12},{13... | collective-permute-start | bytes 46088 | tf_op jit(solution)/shard_map/ppermute | solution.py:432
  22.1 2.8 %collective-permute-start.3 = (f32[30,128]{1,0:T(8,128)S(1)}, f32[30,128]{1,0:T(8,128)S(1)}, u32[]{:S(2)}, u32[]{:S(2)}) collective-permute-start(f32[30,128]{1,0:T(8,128)S(1)} %get-tuple-element.31), channel_id=1, source_target_pairs={{0,1},{2,3},{4,5},{6,7},{1,0},{3,2},{5,4},{7,6},{8,9},{10,11},{12,... | collective-permute-start | bytes 46088 | tf_op jit(solution)/shard_map/ppermute | solution.py:432
